TPU v7x, 512 devices: a whole 4x8x8 slice. The times are simulated.
512 devices in a mesh: leaf: 128 (over y, z, core), rep: 4 (over x).
Axes of the slice: x: 4, y: 8, z: 8, core: 2. Of those that a mesh axis runs over, the one named last changes fastest.
Arguments:
- bottom_factor: float32 [512, 4096], P('leaf'), may hold values from -1 to 3, as said below
- transfer0: float32 [512, 4096], P('leaf'), may hold values from -0.3 to 1, as said below
- transfer1: float32 [256, 4096], P('leaf'), may hold values from -0.3 to 1, as said below
- transfer2: float32 [128, 4096], P('leaf'), may hold values from -0.3 to 1, as said below
- transfer3: float32 [64, 4096], replicated, may hold values from -0.3 to 1, as said below
- child_order: int32 [128, 4], P('leaf'), may hold values from 0 to 3, each once within a row
- coupling: bfloat16 [98304, 4096], P(('leaf', 'rep')), may hold values from -4 to 4
- admissible: int32 [3, 98304], P(None, ('leaf', 'rep')), may hold values from 0 to 511, as said below
Outputs:
- projected: bfloat16 [98304, 4096], P(('leaf', 'rep'))
- gram0: float32 [512, 4096], P('leaf')
- gram1: float32 [256, 4096], P('leaf')
- gram2: float32 [128, 4096], P('leaf')
Inputs may be any that keep to these rules, and one draw needn't show every extreme that they name: `bottom_factor`: each row is an upper-triangular 64 x 64 matrix with positive diagonal. `transfer0`: rows are 64 x 64 matrices. `transfer1`: rows are 64 x 64 matrices. `transfer2`: rows are 64 x 64 matrices. `transfer3`: rows are 64 x 64 matrices. `admissible`: entry (0, b) is a level 0 to 4. With l = b // (192 times the size of rep): entry (1, b) is a cluster of that level numbered from 0, at levels 0 to 2 one of the 4 / 2^level clusters starting at l * 4 / 2^level, at level 3 cluster l // 2, at level 4 cluster l // 4; entry (2, b) at levels 0 to 2 is another cluster of that level held in the same way by leaf index l - 1, l or l + 1, at levels 3 and 4 the row cluster's sibling (its number XOR 1).
All inputs are finite; a program needn't handle non-finite values.
Results may differ from a plain program's by a relative error of at most 0.0064.
Values may be sent and summed in bfloat16 or wider, within the bound.
A program may use at most 64 MiB of HBM per device.

v0:
```python
import jax
import jax.numpy as jnp
from jax import lax
from jax.sharding import PartitionSpec as P

RANK = 64
CL_DEV = 4


HIGHEST_PRECISION = lax.Precision.HIGHEST


def padded(block, sides, width):
    for axis, dim in sides:
        count = lax.axis_size(axis)
        forward = [(i, i + 1) for i in range(count - 1)]
        backward = [(target, source) for source, target in forward]
        low = lax.ppermute(
            lax.slice_in_dim(block, block.shape[dim] - width, None, axis=dim), axis, forward
        )
        high = lax.ppermute(lax.slice_in_dim(block, 0, width, axis=dim), axis, backward)
        block = jnp.concatenate([low, block, high], axis=dim)
    return block


def from_partner(value, axis, distance):
    return lax.ppermute(value, axis, [(i, i ^ 1 << distance) for i in range(lax.axis_size(axis))])


def squares(flat):
    return flat.reshape(-1, RANK, RANK)


def apply_transfer(factors, transfers):
    return jnp.einsum("cij,cjk->cik", factors, transfers, precision=HIGHEST_PRECISION)


def upper_factor(gram):
    lower = jnp.linalg.cholesky(gram)
    return jnp.swapaxes(lower, 1, 2)


def merge_pair(first_kid, second_kid):
    gram = jnp.einsum("cki,ckj->cij", first_kid, first_kid, precision=HIGHEST_PRECISION)
    gram = gram + jnp.einsum("cki,ckj->cij", second_kid, second_kid, precision=HIGHEST_PRECISION)
    return upper_factor(gram)


def local(
    bottom_factor, transfer0, transfer1, transfer2, transfer3, child_order, coupling, admissible
):
    leaf_index = lax.axis_index("leaf")
    slots = CL_DEV + CL_DEV // 2 + 1
    level_zero = squares(bottom_factor)
    images_zero = apply_transfer(level_zero, squares(transfer0))
    children = child_order.reshape(-1)
    level_one = merge_pair(images_zero[children[0::2]], images_zero[children[1::2]])
    images_one = apply_transfer(level_one, squares(transfer1))
    level_two = merge_pair(images_one[0::2], images_one[1::2])
    images_two = apply_transfer(level_two, squares(transfer2))
    upper_transfers = squares(transfer3)
    local_factors = jnp.concatenate([level_zero, level_one, level_two]).astype(jnp.bfloat16)
    nearby = padded(local_factors.reshape(1, slots, RANK * RANK), (("leaf", 0),), 1)
    partner_two = from_partner(images_two, "leaf", 0)
    even_side = leaf_index % 2 == 0
    level_three = merge_pair(
        jnp.where(even_side, images_two, partner_two), jnp.where(even_side, partner_two, images_two)
    )
    own_transfer = lax.dynamic_slice_in_dim(upper_transfers, leaf_index // 2, 1, 0)
    images_three = apply_transfer(level_three, own_transfer)
    three_rounded = level_three.astype(jnp.bfloat16)
    partner_three, partner_factor = (
        from_partner(images_three, "leaf", 1),
        from_partner(three_rounded.astype(jnp.float32), "leaf", 1).astype(three_rounded.dtype),
    )
    even_pair = leaf_index // 2 % 2 == 0
    level_four = merge_pair(
        jnp.where(even_pair, images_three, partner_three),
        jnp.where(even_pair, partner_three, images_three),
    )
    four_rounded = level_four.astype(jnp.bfloat16)
    partner_four = from_partner(four_rounded, "leaf", 2)
    upper_table = jnp.concatenate([three_rounded, partner_factor, four_rounded, partner_four])
    factor_table = jnp.concatenate([squares(nearby), upper_table])
    levels = admissible[0]
    per_leaf = jnp.maximum(CL_DEV // jnp.left_shift(1, levels), 1)
    level_base = jnp.where(levels == 0, 0, jnp.where(levels == 1, CL_DEV, CL_DEV + CL_DEV // 2))
    lower_count = 3 * slots

    def locate(cluster, column_side):
        low_place = (cluster // per_leaf - leaf_index + 1) * slots + level_base + cluster % per_leaf
        high_place = jnp.where(
            levels == 3, lower_count + column_side, lower_count + 2 + column_side
        )
        return jnp.where(levels <= 2, low_place, high_place)

    row_factors = factor_table[locate(admissible[1], 0)]
    column_factors = factor_table[locate(admissible[2], 1)]
    blocks = squares(coupling)
    half_product = jnp.einsum(
        "bij,bjk->bik", row_factors, blocks, preferred_element_type=jnp.float32
    ).astype(jnp.bfloat16)
    result = jnp.einsum(
        "bik,blk->bil", half_product, column_factors, preferred_element_type=jnp.float32
    )
    gram_terms = jnp.einsum("bil,bml->bim", result, result, precision=HIGHEST_PRECISION) / RANK
    gram_slot = jnp.where(levels <= 2, level_base + admissible[1] % per_leaf, -1)
    selector = (gram_slot[:, None] == jnp.arange(slots, dtype=jnp.int32)[None, :]).astype(
        jnp.float32
    )
    partial_sums = jnp.einsum(
        "bk,bx->kx", selector, gram_terms.reshape(-1, RANK * RANK), precision=HIGHEST_PRECISION
    )
    totals = lax.psum(partial_sums, "rep")
    return (
        result.astype(jnp.bfloat16).reshape(-1, RANK * RANK),
        totals[:CL_DEV],
        totals[CL_DEV : CL_DEV + CL_DEV // 2],
        totals[CL_DEV + CL_DEV // 2 :],
    )


def solution(mesh):
    return jax.shard_map(
        local,
        mesh=mesh,
        in_specs=(
            P("leaf", None),
            P("leaf", None),
            P("leaf", None),
            P("leaf", None),
            P(),
            P("leaf", None),
            P(("leaf", "rep"), None),
            P(None, ("leaf", "rep")),
        ),
        out_specs=(P(("leaf", "rep"), None), P("leaf", None), P("leaf", None), P("leaf", None)),
        check_vma=False,
    )
```

profile of v0, /device:TPU:16, one launch (start us, length us, event | category | flops | bytes accessed | tf_op | source)
XLA Modules:
  0.0 203.4 jit_solution(14578983610700379295)
XLA Ops:
  7.2 0.8 slice.44
  8.1 0.7 slice.43
  8.8 0.9 convert_bitcast_fusion
  9.7 1.0 reshape.539
  10.7 0.9 reshape.542
  11.5 1.0 reshape.540
  14.6 11.7 %custom-call.7 = f32[2,64,64]{2,1,0:T(8,128)S(1)} custom-call(f32[2,64,64]{2,1,0:T(8,128)S(1)} %fusion.5), custom_call_target="Cholesky" | custom-call | tf_op jit(solution)/shard_map/jit(cholesky)/cholesky | solution.py:39
  27.7 5.8 %custom-call.10 = f32[1,64,64]{2,1,0:T(8,128)S(1)} custom-call(f32[1,64,64]{2,1,0:T(8,128)S(1)} %fusion.15), custom_call_target="Cholesky" | custom-call | tf_op jit(solution)/shard_map/jit(cholesky)/cholesky | solution.py:39
  34.3 0.7 fusion.37
  35.2 10.3 %collective-permute-start.1 = (bf16[1,7,4096]{2,1,0:T(8,128)(2,1)S(1)}, bf16[1,7,4096]{2,1,0:T(8,128)(2,1)S(1)}, u32[]{:S(2)}, u32[]{:S(2)}) collective-permute-start(bf16[1,7,4096]{2,1,0:T(8,128)(2,1)S(1)} %pad_maximum_fusion.1), channel_id=1, source_target_pairs={{4,0},{8,4},{12,8},{16,12},{20,16},{24,20},{28,24},{32,28},{36,32}... | collective-permute-start | bytes 172040 | tf_op jit(solution)/shard_map/ppermute | solution.py:21
  45.5 1.9 collective-permute-start
  47.9 0.7 reduce.20
  48.7 0.9 convolution_bitcast_fusion.1
  49.6 1.9 collective-permute-start.2
  52.3 0.7 fusion.56
  53.0 0.8 reshape.551
  54.4 5.8 %custom-call.11 = f32[1,64,64]{2,1,0:T(8,128)S(1)} custom-call(f32[1,64,64]{2,1,0:T(8,128)S(1)} %fusion.14), custom_call_target="Cholesky" | custom-call | tf_op jit(solution)/shard_map/jit(cholesky)/cholesky | solution.py:39
  61.0 0.9 convolution_bitcast_fusion
  61.9 1.9 collective-permute-start.4
  63.8 0.7 fusion.36
  64.5 3.9 %collective-permute-start.3 = (bf16[1,64,64]{1,2,0:T(8,128)(2,1)S(1)}, bf16[1,64,64]{1,2,0:T(8,128)(2,1)S(1)}, u32[]{:S(2)}, u32[]{:S(2)}) collective-permute-start(bf16[1,64,64]{1,2,0:T(8,128)(2,1)S(1)} %fusion.36), channel_id=1, source_target_pairs={{0,8},{4,12},{8,0},{12,4},{16,24},{20,28},{24,16},{28,20},{32,40},... | collective-permute-start | bytes 24584 | tf_op jit(solution)/shard_map/ppermute | solution.py:27
  69.0 5.8 %custom-call.12 = f32[1,64,64]{2,1,0:T(8,128)S(1)} custom-call(f32[1,64,64]{2,1,0:T(8,128)S(1)} %fusion.13), custom_call_target="Cholesky" | custom-call | tf_op jit(solution)/shard_map/jit(cholesky)/cholesky | solution.py:39
  75.5 0.7 fusion.38
  76.2 2.1 %collective-permute-start.5 = (bf16[1,64,64]{1,2,0:T(8,128)(2,1)S(1)}, bf16[1,64,64]{1,2,0:T(8,128)(2,1)S(1)}, u32[]{:S(2)}, u32[]{:S(2)}) collective-permute-start(bf16[1,64,64]{1,2,0:T(8,128)(2,1)S(1)} %fusion.38), channel_id=1, source_target_pairs={{0,16},{4,20},{8,24},{12,28},{16,0},{20,4},{24,8},{28,12},{32,48},... | collective-permute-start | bytes 24584 | tf_op jit(solution)/shard_map/ppermute | solution.py:27
  78.9 3.9 %copy.77 = bf16[192,4096]{0,1:T(8,128)(2,1)} copy(bf16[192,4096]{1,0:T(8,128)(2,1)} %param.15) | data formatting | bytes 3145728 | tf_op args[6]
  82.8 4.2 %copy.78 = bf16[192,64,64]{2,1,0:T(8,128)(2,1)S(1)} copy(bf16[192,64,64]{0,2,1:T(8,128)(2,1)} %bitcast.158) | data formatting | bytes 3145728 | tf_op jit(solution)/shard_map/reshape | solution.py:31
  87.0 0.7 copy.73
  87.7 0.7 copy.74
  88.4 0.7 copy.75
  89.1 0.7 copy.76
  89.8 1.1 reshape.545
  90.9 1.0 constant_dynamic-update-slice_fusion.4
  91.9 0.7 constant_dynamic-update-slice_fusion.3
  92.7 0.7 constant_dynamic-update-slice_fusion.2
  93.4 0.7 constant_dynamic-update-slice_fusion.1
  94.1 0.7 constant_dynamic-update-slice_fusion
  94.8 2.9 %gather_fusion.3 = bf16[192,64,64]{2,1,0:T(8,128)(2,1)} fusion(bf16[25,64,64]{2,1,0:T(8,128)(2,1)S(1)} %constant_dynamic-update-slice_fusion, s32[1024]{0:T(1024)} %get-tuple-element.21), kind=kCustom, calls=%fused_computation.3 | custom fusion | bytes 3146496 | tf_op jit(solution)/shard_map/gather | solution.py:98
  97.7 2.8 %gather_fusion.2 = bf16[192,64,64]{2,1,0:T(8,128)(2,1)} fusion(bf16[25,64,64]{2,1,0:T(8,128)(2,1)S(1)} %constant_dynamic-update-slice_fusion, s32[1024]{0:T(1024)} %get-tuple-element.22), kind=kCustom, calls=%fused_computation.2 | custom fusion | bytes 3146496 | tf_op jit(solution)/shard_map/gather | solution.py:97
  100.5 9.1 %fusion.67 = (bf16[192,64,64]{2,1,0:T(8,128)(2,1)}, f32[192,64,64]{2,1,0:T(8,128)}) fusion(bf16[192,64,64]{2,1,0:T(8,128)(2,1)} %gather_fusion.3, bf16[192,64,64]{2,1,0:T(8,128)(2,1)} %gather_fusion.2, bf16[192,64,64]{2,1,0:T(8,128)(2,1)S(1)} %copy.78), kind=kOutput, calls=%fused_computation.139 | convolution fusion | flops 202899456 | bytes 9437184 | tf_op jit(solution)/shard_map/bik,blk->bil/dot_general | solution.py:103
  109.6 16.4 %broadcast_multiply_fusion = f32[192,64,64]{2,1,0:T(8,128)} fusion(f32[192,64,64]{2,1,0:T(8,128)} %get-tuple-element.20), kind=kOutput, calls=%fused_computation.4 | convolution fusion | flops 604766208 | bytes 6291456 | tf_op jit(solution)/shard_map/bil,bml->bim/dot_general | solution.py:106
  126.1 6.7 %copy.80 = f32[192,64,64]{0,2,1:T(8,128)} copy(f32[192,64,64]{2,1,0:T(8,128)} %broadcast_multiply_fusion) | data formatting | bytes 6291456 | tf_op jit(solution)/shard_map/div | solution.py:106
  132.8 5.0 %fusion.8 = f32[7,4096]{1,0:T(8,128)} fusion(f32[192,4096]{0,1:T(8,128)} %bitcast.156, s32[192]{0:T(256)S(1)} %copy-done.4), kind=kOutput, calls=%fused_computation.24 | convolution fusion | flops 66062976 | bytes 3261184 | tf_op jit(solution)/shard_map/bk,bx->kx/dot_general | solution.py:111
  137.8 3.8 %copy.79 = bf16[192,64,64]{0,2,1:T(8,128)(2,1)} copy(bf16[192,64,64]{2,1,0:T(8,128)(2,1)S(1)} %copy-done) | data formatting | bytes 3145728 | tf_op jit(solution)/shard_map/convert_element_type | solution.py:116
  141.6 3.9 %copy.81 = bf16[192,4096]{1,0:T(8,128)(2,1)} copy(bf16[192,4096]{0,1:T(8,128)(2,1)} %bitcast.157) | data formatting | bytes 3145728
  145.5 46.5 %all-reduce.2.cloned.1.call-done = f32[7,4096]{1,0:T(8,128)} async-done(((f32[7,4096]{1,0:T(8,128)}), f32[7,4096]{1,0:T(8,128)}) %all-reduce.2.cloned.1.call-update) | async-done | bytes 114704 | tf_op jit(solution)/shard_map/psum | solution.py:114
  192.0 1.5 slice.65
  193.5 1.5 slice.64
  195.0 1.5 slice.63
  (65 shorter events, 9.0 us)
Async XLA Ops:
  7.2 40.7 %copy-start.2 = (f32[1,4096]{1,0:T(1,128)S(1)}, f32[1,4096]{1,0:T(1,128)}, u32[]{:S(2)}) copy-start(f32[1,4096]{1,0:T(1,128)} %param.12) | copy-start | bytes 49156
  7.2 44.3 %copy-start.3 = (s32[3,192]{1,0:T(4,128)S(1)}, s32[3,192]{1,0:T(4,128)}, u32[]{:S(2)}) copy-start(s32[3,192]{1,0:T(4,128)} %param.16) | copy-start | bytes 6916
  7.2 45.8 %copy-start.1 = (f32[64,4096]{1,0:T(8,128)S(1)}, f32[64,4096]{1,0:T(8,128)}, u32[]{:S(2)}) copy-start(f32[64,4096]{1,0:T(8,128)} %param.13) | copy-start | bytes 3145732
  7.2 184.8 %all-reduce.2.cloned.1.call-start = ((), (), s32[]{:S(2)}) async-start(), calls=%async_computation | async-start | bytes 262144 | tf_op jit(solution)/shard_map/psum | solution.py:114
  35.2 54.6 %collective-permute-start.1 = (bf16[1,7,4096]{2,1,0:T(8,128)(2,1)S(1)}, bf16[1,7,4096]{2,1,0:T(8,128)(2,1)S(1)}, u32[]{:S(2)}, u32[]{:S(2)}) collective-permute-start(bf16[1,7,4096]{2,1,0:T(8,128)(2,1)S(1)} %pad_maximum_fusion.1), channel_id=1, source_target_pairs={{4,0},{8,4},{12,8},{16,12},{20,16},{24,20},{28,24},{32,28},{36,32}... | collective-permute-start | bytes 172040 | tf_op jit(solution)/shard_map/ppermute | solution.py:21
  45.5 44.3 %collective-permute-start = (bf16[1,7,4096]{2,1,0:T(8,128)(2,1)S(1)}, bf16[1,7,4096]{2,1,0:T(8,128)(2,1)S(1)}, u32[]{:S(2)}, u32[]{:S(2)}) collective-permute-start(bf16[1,7,4096]{2,1,0:T(8,128)(2,1)S(1)} %pad_maximum_fusion.1), channel_id=1, source_target_pairs={{0,4},{4,8},{8,12},{12,16},{16,20},{20,24},{24,28},{28,32},{32,36}... | collective-permute-start | bytes 172040 | tf_op jit(solution)/shard_map/ppermute | solution.py:18
  49.6 4.3 %collective-permute-start.2 = (f32[1,64,64]{2,1,0:T(8,128)S(1)}, f32[1,64,64]{2,1,0:T(8,128)S(1)}, u32[]{:S(2)}, u32[]{:S(2)}) collective-permute-start(f32[1,64,64]{2,1,0:T(8,128)S(1)} %convolution_bitcast_fusion.1), channel_id=1, source_target_pairs={{0,4},{4,0},{8,12},{12,8},{16,20},{20,16},{24,28},{28,24},{32,36},... | collective-permute-start | bytes 49160 | tf_op jit(solution)/shard_map/ppermute | solution.py:27
  61.9 6.5 %collective-permute-start.4 = (f32[1,64,64]{2,1,0:T(8,128)S(1)}, f32[1,64,64]{2,1,0:T(8,128)S(1)}, u32[]{:S(2)}, u32[]{:S(2)}) collective-permute-start(f32[1,64,64]{2,1,0:T(8,128)S(1)} %convolution_bitcast_fusion), channel_id=1, source_target_pairs={{0,8},{4,12},{8,0},{12,4},{16,24},{20,28},{24,16},{28,20},{32,40},... | collective-permute-start | bytes 49160 | tf_op jit(solution)/shard_map/ppermute | solution.py:27
  64.5 23.2 %collective-permute-start.3 = (bf16[1,64,64]{1,2,0:T(8,128)(2,1)S(1)}, bf16[1,64,64]{1,2,0:T(8,128)(2,1)S(1)}, u32[]{:S(2)}, u32[]{:S(2)}) collective-permute-start(bf16[1,64,64]{1,2,0:T(8,128)(2,1)S(1)} %fusion.36), channel_id=1, source_target_pairs={{0,8},{4,12},{8,0},{12,4},{16,24},{20,28},{24,16},{28,20},{32,40},... | collective-permute-start | bytes 24584 | tf_op jit(solution)/shard_map/ppermute | solution.py:27
  76.2 12.9 %collective-permute-start.5 = (bf16[1,64,64]{1,2,0:T(8,128)(2,1)S(1)}, bf16[1,64,64]{1,2,0:T(8,128)(2,1)S(1)}, u32[]{:S(2)}, u32[]{:S(2)}) collective-permute-start(bf16[1,64,64]{1,2,0:T(8,128)(2,1)S(1)} %fusion.38), channel_id=1, source_target_pairs={{0,16},{4,20},{8,24},{12,28},{16,0},{20,4},{24,8},{28,12},{32,48},... | collective-permute-start | bytes 24584 | tf_op jit(solution)/shard_map/ppermute | solution.py:27
  126.0 6.7 %copy-start.4 = (s32[192]{0:T(256)S(1)}, s32[192]{0:T(256)}, u32[]{:S(2)}) copy-start(s32[192]{0:T(256)} %fusion.56) | copy-start | bytes 2308
  132.8 5.1 %copy-start = (bf16[192,64,64]{2,1,0:T(8,128)(2,1)S(1)}, bf16[192,64,64]{2,1,0:T(8,128)(2,1)}, u32[]{:S(2)}) copy-start(bf16[192,64,64]{2,1,0:T(8,128)(2,1)} %get-tuple-element.19) | copy-start | bytes 4718596
Sparse Core Ops, SparseCore 0:
  137.9 53.9 all-reduce.1
where the time goes:
time: 205 us; the launch traced here: 203 us
  local copies, waits for them, and re-layouts  48.1 us (23%)
  waiting for transfers between devices  46.5 us (23%)
  other arithmetic  37.4 us (18%)
  matrix products  34.9 us (17%)
  starting transfers between devices  22.1 us (11%)
  between operations  14.4 us (7%)
    psum x1, waiting for transfers between devices, local(): totals = lax.psum(partial_sums, 'rep')  46.5 us
    another operation x13, other arithmetic, upper_factor(): lower = jnp.linalg.cholesky(gram)  31.4 us
    dot_general x1, matrix products, local(): jnp.einsum('bil,bml->bim', result, result, precision=HIGHEST_PRECISION)  16.4 us
    unnamed x17, local copies, waits for them, and re-layouts  11.5 us
    ppermute x1, starting transfers between devices, padded(): lax.ppermute(lax.slice_in_dim(block, 0, width, axis=dim), axis, backward)  10.3 us
    ppermute x4, starting transfers between devices, from_partner(): lax.ppermute(value, axis, [(i, i ^ 1 << distance) for i in range(lax.axis...  9.86 us
    dot_general x1, matrix products, local(): jnp.einsum('bik,blk->bil', half_product, column_factors, preferred_elemen...  9.06 us
    reshape x6, local copies, waits for them, and re-layouts, squares(): return flat.reshape(-1, RANK, RANK)  8.92 us
  transfers between devices with their start and end apart: 7, of which 1 were waited for; matrix products, arithmetic and copies ran while one was open for 20% of the time, Pallas kernels for 0%

commit v1 on v0

v1 whole, which is shorter than its diff:
```python
import functools

import jax
import jax.numpy as jnp
from jax import lax
from jax.experimental import pallas as pl
from jax.experimental.pallas import tpu as pltpu
from jax.sharding import PartitionSpec as P

RANK = 64
HALF = 32
LANES = 128
FLAT = RANK * RANK
CL_DEV = 4
SLOTS = 7
ROW_SLOTS = 9
COLUMNS = 3 * SLOTS + 2
GROUP = 8
MESH = pl.DeviceIdType.MESH
F32 = jnp.float32
BF16 = jnp.bfloat16
EXACT = lax.Precision.HIGHEST
MIB = 1024 * 1024


def lanes_left(rows):
    return lax.broadcasted_iota(jnp.int32, (rows, LANES), 1) < RANK


def swap(x):
    return pltpu.roll(x, RANK, 1)


def exact_dot(a, b):
    return jnp.dot(a, b, precision=EXACT, preferred_element_type=F32)


def exact_gram(a, b):
    return lax.dot_general(a, b, (((0,), (0,)), ((), ())), precision=EXACT, preferred_element_type=F32)


def flipped(index, bits):
    result = index
    for place in range(3):
        if bits >> place & 1:
            result = result + (1 - 2 * (index // (1 << place) % 2)) * (1 << place)
    return result


def tiles_of(flat, rows, lines):
    for tile in range(HALF):
        lines[tile * 8 : tile * 8 + rows, :] = flat[:, tile * LANES : (tile + 1) * LANES]


def packed(lines, which):
    return lines[pl.ds(which, HALF, stride=8), :]


def natural_pair(left, right, page):
    side = lanes_left(HALF)
    page[pl.ds(0, HALF, stride=2), :] = jnp.where(side, left, swap(right))
    page[pl.ds(1, HALF, stride=2), :] = jnp.where(side, swap(left), right)
    return page[...]


def pack(x):
    return jnp.concatenate([x[:HALF], x[HALF:]], axis=1)


def unpack(x):
    return jnp.concatenate([x[:, :RANK], x[:, RANK:]], axis=0)


def upsweep_kernel(
    leaves, chunk,
    order, bottom, zero, one, two, three,
    grams_out, factors_out,
    lines, lines_three, flat_three, page, kids, factors, pairs, tops, images,
    three_sem, send, receive,
):
    me = lax.axis_index("leaf")
    rep = lax.axis_index("rep")
    left = lax.rem(me + leaves - 1, leaves)
    right = lax.rem(me + 1, leaves)
    others = [flipped(me, bits) for bits in range(1, GROUP)]
    barrier = pltpu.get_barrier_semaphore()
    for other in [left, right] + others:
        pl.semaphore_signal(barrier, inc=1, device_id=(other, rep), device_id_type=MESH)
    start = pl.multiple_of(me // 2 // chunk * chunk, chunk)
    fetch = pltpu.make_async_copy(three.at[pl.ds(start, chunk)], flat_three, three_sem)
    fetch.start()

    tiles_of(bottom, CL_DEV, lines)
    bottoms = [packed(lines, c) for c in range(CL_DEV)]
    leaf_pairs = [natural_pair(bottoms[c], bottoms[c + 1], page) for c in (0, 2)]
    for k in range(2):
        factors[1, k * RANK : (k + 1) * RANK, :] = leaf_pairs[k].astype(BF16)
    tiles_of(zero, CL_DEV, lines)
    zeros = [packed(lines, c) for c in range(CL_DEV)]
    zero_pairs = [natural_pair(zeros[c], zeros[c + 1], page) for c in (0, 2)]
    tiles_of(one, CL_DEV // 2, lines)
    ones = natural_pair(packed(lines, 0), packed(lines, 1), page)
    tiles_of(two, 1, lines)
    own_two = packed(lines, 0)
    twos = natural_pair(own_two, own_two, page)[:, :RANK]

    for c in range(CL_DEV):
        half = slice(c % 2 * RANK, c % 2 * RANK + RANK)
        image = exact_dot(leaf_pairs[c // 2][:, half], zero_pairs[c // 2][:, half])
        kids[c] = exact_gram(image, image)
    level_one = [kids[order[0, 2 * i]] + kids[order[0, 2 * i + 1]] for i in range(2)]
    pairs[1, :RANK, :] = jnp.concatenate(level_one, axis=1)
    level_two = 0.0
    for i in range(2):
        transfer = ones[:, i * RANK : (i + 1) * RANK]
        level_two = level_two + exact_gram(transfer, exact_dot(level_one[i], transfer))
    pairs[1, RANK:, :] = pack(level_two)
    tops[0] = pack(exact_gram(twos, exact_dot(level_two, twos)))

    pl.semaphore_wait(barrier, GROUP + 1)
    copies = []

    def push(source, target, device):
        place = len(copies)
        copy = pltpu.make_async_remote_copy(
            src_ref=source, dst_ref=target, send_sem=send.at[place], recv_sem=receive.at[place],
            device_id=(device, rep), device_id_type=MESH,
        )
        copy.start()
        copies.append(copy)

    for bits in range(1, GROUP):
        push(tops.at[0], tops.at[bits], others[bits - 1])
    push(pairs.at[1], pairs.at[2], left)
    push(pairs.at[1], pairs.at[0], right)
    push(factors.at[1], factors.at[2], left)
    push(factors.at[1], factors.at[0], right)

    fetch.wait()
    tiles_of(flat_three, chunk, lines_three)
    place = lax.rem(me // 2, chunk)
    threes = []
    for u in range(GROUP // 2):
        own = packed(lines_three, flipped(place, u))
        threes.append(natural_pair(own, own, page)[:, :RANK])
    for copy in copies[: GROUP - 1]:
        copy.wait_recv()
    level_three, lifted = [], []
    for u in range(GROUP // 2):
        gram = unpack(tops[2 * u] + tops[2 * u + 1])
        level_three.append(gram)
        lifted.append(exact_gram(threes[u], exact_dot(gram, threes[u])))
    level_four = [lifted[0] + lifted[1], lifted[2] + lifted[3]]
    for copy in copies[GROUP - 1 :]:
        copy.wait_recv()
    for side in range(3):
        grams_out[side * RANK : (side + 1) * RANK, :] = pairs[side, :RANK, :]
        factors_out[side * LANES : (side + 1) * LANES, :] = factors[side]
    side_two = [unpack(pairs[side, RANK:, :]) for side in range(3)]
    rest = side_two + [level_three[0], level_three[1], level_four[0], level_four[1], level_four[1]]
    for k in range(4):
        at = (3 + k) * RANK
        grams_out[at : at + RANK, :] = jnp.concatenate([rest[2 * k], rest[2 * k + 1]], axis=1)
    grams_out[7 * RANK :, :] = pairs[1, :RANK, :]
    for copy in copies:
        copy.wait_send()


def upsweep(leaves, order, bottom, zero, one, two, three):
    chunk = min(8, three.shape[0])
    vmem = pl.BlockSpec(memory_space=pltpu.VMEM)
    count = GROUP + 3
    return pl.pallas_call(
        functools.partial(upsweep_kernel, leaves, chunk),
        out_shape=[
            jax.ShapeDtypeStruct((8 * RANK, LANES), F32),
            jax.ShapeDtypeStruct((3 * LANES, LANES), BF16),
        ],
        in_specs=[pl.BlockSpec(memory_space=pltpu.SMEM)] + [vmem] * 4 + [pl.BlockSpec(memory_space=pl.ANY)],
        out_specs=[vmem, vmem],
        scratch_shapes=[
            pltpu.VMEM((HALF * 8, LANES), F32),
            pltpu.VMEM((HALF * 8, LANES), F32),
            pltpu.VMEM((chunk, FLAT), F32),
            pltpu.VMEM((RANK, LANES), F32),
            pltpu.VMEM((CL_DEV, RANK, RANK), F32),
            pltpu.VMEM((3, LANES, LANES), BF16),
            pltpu.VMEM((3, RANK + HALF, LANES), F32),
            pltpu.VMEM((GROUP, HALF, LANES), F32),
            pltpu.VMEM((8, LANES), F32),
            pltpu.SemaphoreType.DMA,
            pltpu.SemaphoreType.DMA((count,)),
            pltpu.SemaphoreType.DMA((count,)),
        ],
        compiler_params=pltpu.CompilerParams(
            collective_id=0, has_side_effects=True, vmem_limit_bytes=32 * MIB
        ),
        name="upsweep",
    )(order, bottom, zero, one, two, three)


def picked(x, index):
    return jnp.take_along_axis(x, index, axis=1, mode="promise_in_bounds")


def factorize(rows):
    lane = lax.broadcasted_iota(jnp.int32, (8, LANES), 1)
    base = jnp.where(lane < RANK, 0, RANK)
    inner = lane - base
    rows = list(rows)
    result = []
    for panel in range(0, RANK, 8):
        entry = {}
        for r in range(8):
            for c in range(r, 8):
                entry[r, c] = picked(rows[panel + r], base + (panel + c))
        done = []
        for k in range(8):
            scale = lax.rsqrt(entry[k, k])
            done.append(rows[panel + k] * scale)
            for c in range(k + 1, 8):
                entry[k, c] = entry[k, c] * scale
            for r in range(k + 1, 8):
                rows[panel + r] = rows[panel + r] - entry[k, r] * done[k]
                for c in range(r, 8):
                    entry[r, c] = entry[r, c] - entry[k, r] * entry[k, c]
        for i in range(panel + 8, RANK):
            for k in range(8):
                rows[i] = rows[i] - picked(done[k], base + i) * done[k]
        for k in range(8):
            result.append(jnp.where(inner >= panel + k, done[k], 0.0))
    return result


def visit_order(admissible, leaf, padded_in):
    wide = 256
    padded_in[...] = jnp.full(padded_in.shape, -1, jnp.int32)
    padded_in[0:3, 0 : admissible.shape[1]] = admissible[...]
    level = padded_in[0:1, :]
    row = padded_in[1:2, :]
    column = padded_in[2:3, :]
    low = level <= 2
    base = jnp.where(level == 0, 0, jnp.where(level == 1, CL_DEV, CL_DEV + CL_DEV // 2))
    shift = jnp.where(level == 0, 2, jnp.where(level == 1, 1, 0))
    held = jnp.left_shift(1, shift) - 1
    slot = jnp.where(low, base + jnp.bitwise_and(row, held), level + (SLOTS - 3))
    slot = jnp.where(level < 0, -1, slot)
    side = jnp.clip(jnp.right_shift(column, shift) - leaf + 1, 0, 2)
    place = jnp.where(
        low, side * SLOTS + base + jnp.bitwise_and(column, held), 3 * SLOTS + level - 3
    )
    member = lax.broadcasted_iota(jnp.int32, (16, wide), 0) == slot
    ahead = lax.broadcasted_iota(jnp.int32, (wide, wide), 0) <= lax.broadcasted_iota(
        jnp.int32, (wide, wide), 1
    )
    member_f = jnp.where(member, 1.0, 0.0).astype(F32)
    rank = jnp.dot(member_f.astype(BF16), jnp.where(ahead, 1.0, 0.0).astype(BF16), preferred_element_type=F32)
    count = jnp.sum(member_f, axis=1, keepdims=True)
    even = jnp.floor((count + 1.0) * 0.5) * 2.0
    even = jnp.broadcast_to(even, (16, wide)).astype(BF16)
    below = lax.broadcasted_iota(jnp.int32, (16, 16), 1) < lax.broadcasted_iota(jnp.int32, (16, 16), 0)
    begin = jnp.dot(jnp.where(below, 1.0, 0.0).astype(BF16), even, preferred_element_type=F32)
    at = jnp.sum(jnp.where(member, begin + rank - 1.0, 0.0), axis=0, keepdims=True)
    at = jnp.where(slot < 0, -1.0, at).astype(jnp.int32)
    chosen = lax.broadcasted_iota(jnp.int32, (wide, wide), 0) == at
    line = lax.broadcasted_iota(jnp.int32, (8, wide), 0)
    number = lax.broadcasted_iota(jnp.int32, (8, wide), 1) + 1
    values = jnp.where(line == 0, number, jnp.where(line == 1, place, jnp.where(line == 2, slot, 0)))
    return lax.dot_general(
        values.astype(F32).astype(BF16), jnp.where(chosen, 1.0, 0.0).astype(BF16),
        (((1,), (1,)), ((), ())), preferred_element_type=F32,
    ).astype(jnp.int32)


def blocks_kernel(
    blocks, pairs,
    admissible, grams, leaf_factors, coupling,
    projected, weights_out,
    padded_in, order_v, order, lines, upper, row_table, column_left, column_right,
    own, turned, results, totals, order_sem,
):
    leaf = lax.axis_index("leaf")
    side = lanes_left(HALF)
    side_full = lanes_left(RANK)
    lane = lax.broadcasted_iota(jnp.int32, (RANK, LANES), 1)
    inner = jnp.where(lane < RANK, lane, lane - RANK)
    spread = jnp.where(inner < HALF, 2 * inner, 2 * inner - (RANK - 1)) + (lane - inner)

    order_v[...] = visit_order(admissible, leaf, padded_in)
    to_scalar = pltpu.make_async_copy(order_v, order, order_sem)
    to_scalar.start()

    own[0] = jnp.zeros((HALF, LANES), BF16)
    turned[0] = jnp.zeros((HALF, LANES), BF16)

    def lay(group, carry):
        first = pl.multiple_of(group * 16, 16)
        x = coupling[pl.ds(first, 16), :].astype(F32)
        for h in range(2):
            for tile in range(HALF):
                at = (h * HALF + tile) * 8
                lines[at : at + 8, :] = x[8 * h : 8 * h + 8, tile * LANES : (tile + 1) * LANES]
        for s in range(16):
            block = lines[pl.ds(s // 8 * 256 + s % 8, HALF, stride=8), :]
            own[first + s + 1] = block.astype(BF16)
            turned[first + s + 1] = swap(block).astype(BF16)
        return carry

    lax.fori_loop(0, blocks // 16, lay, 0)

    rows = factorize([grams[pl.ds(i, 8, stride=RANK), :] for i in range(RANK)])
    for i in range(RANK):
        upper[i * 8 : (i + 1) * 8, :] = rows[i]

    def put_column(where, left, right):
        column_left[where] = left.astype(BF16)
        column_right[where] = right.astype(BF16)

    def put_columns(first, second, names):
        flipped_all = jnp.transpose(jnp.concatenate([first, second], axis=0))
        for half in range(2):
            part = flipped_all[half * RANK : (half + 1) * RANK]
            other = swap(part)
            if names[half] is not None:
                put_column(names[half], jnp.where(side_full, part, 0.0), jnp.where(side_full, 0.0, other))
            if names[2 + half] is not None:
                put_column(names[2 + half], jnp.where(side_full, other, 0.0), jnp.where(side_full, 0.0, part))

    def put_rows(even, odd, names):
        x = picked(jnp.concatenate([even, odd], axis=0), spread)
        if names[0] is not None:
            row_table[names[0]] = x.astype(BF16)
        if names[1] is not None:
            row_table[names[1]] = swap(x).astype(BF16)

    for near in range(3):
        first = leaf_factors[near * LANES : near * LANES + RANK, :].astype(F32)
        second = leaf_factors[near * LANES + RANK : (near + 1) * LANES, :].astype(F32)
        put_columns(first, second, [near * SLOTS + c for c in (0, 1, 2, 3)])
        if near == 1:
            for k, x in enumerate((first, second)):
                lines[k * RANK : (k + 1) * RANK, :] = x
                put_rows(
                    lines[pl.ds(k * RANK, HALF, stride=2), :],
                    lines[pl.ds(k * RANK + 1, HALF, stride=2), :],
                    (2 * k, 2 * k + 1),
                )
    column_names = [
        (4, 5), (SLOTS + 4, SLOTS + 5), (2 * SLOTS + 4, 2 * SLOTS + 5), (6, SLOTS + 6),
        (2 * SLOTS + 6, None), (3 * SLOTS, None), (3 * SLOTS + 1, None), (None, None),
    ]
    for k in range(0, 8, 2):
        put_columns(
            upper[pl.ds(k, RANK, stride=8), :], upper[pl.ds(k + 1, RANK, stride=8), :],
            column_names[k] + column_names[k + 1],
        )
    for k, names in ((1, (4, 5)), (3, (None, 6)), (4, (None, 7)), (5, (None, 8))):
        put_rows(upper[pl.ds(k, HALF, stride=16), :], upper[pl.ds(8 + k, HALF, stride=16), :], names)

    totals[...] = jnp.zeros(totals.shape, F32)
    to_scalar.wait()

    def visit(pair):
        a, b = order[0, 2 * pair], order[0, 2 * pair + 1]
        slot = order[2, 2 * pair]
        both = jnp.concatenate(
            [jnp.where(side, own[a], turned[b]), jnp.where(side, turned[a], own[b])], axis=0
        )
        half = jnp.dot(row_table[slot][:, :RANK], both, preferred_element_type=F32).astype(BF16)
        columns = jnp.concatenate(
            [column_left[order[1, 2 * pair]], column_right[order[1, 2 * pair + 1]]], axis=0
        )
        result = jnp.dot(half, columns, preferred_element_type=F32)
        rounded = result.astype(BF16)
        totals[slot, :, :RANK] += lax.dot_general(
            rounded, rounded, (((1,), (1,)), ((), ())), preferred_element_type=F32
        )
        top, bottom = result[:HALF], result[HALF:]
        results[pl.ds(pl.multiple_of(a * HALF, HALF), HALF), :] = jnp.where(side, top, swap(bottom))
        results[pl.ds(pl.multiple_of(b * HALF, HALF), HALF), :] = jnp.where(side, swap(top), bottom)

    def visits(step, carry):
        for k in range(4):
            visit(step * 4 + k)
        return carry

    lax.fori_loop(0, pairs // 4, visits, 0)

    gather = jnp.where(inner % 2 == 0, inner // 2, HALF + inner // 2)
    for s in range(SLOTS):
        x = picked(totals[s], gather)
        weights_out[s * HALF : (s + 1) * HALF, :] = jnp.where(side, x[:HALF], x[HALF:]) * (1.0 / RANK)

    def write(group, carry):
        first = pl.multiple_of(group * 16, 16)
        for tile in range(HALF):
            at = (first + 1) * HALF + tile
            x = jnp.concatenate(
                [
                    results[pl.ds(at, 8, stride=HALF), :],
                    results[pl.ds(at + 8 * HALF, 8, stride=HALF), :],
                ],
                axis=0,
            )
            projected[pl.ds(first, 16), tile * LANES : (tile + 1) * LANES] = x.astype(BF16)
        return carry

    lax.fori_loop(0, blocks // 16, write, 0)


def blocks_call(admissible, grams, leaf_factors, coupling):
    blocks = coupling.shape[0]
    pairs = -(-(blocks + ROW_SLOTS) // 2)
    pairs = -(-pairs // 4) * 4
    vmem = pl.BlockSpec(memory_space=pltpu.VMEM)
    return pl.pallas_call(
        functools.partial(blocks_kernel, blocks, pairs),
        out_shape=[
            jax.ShapeDtypeStruct((blocks, FLAT), BF16),
            jax.ShapeDtypeStruct((SLOTS * HALF, LANES), F32),
        ],
        in_specs=[vmem] * 4,
        out_specs=[vmem] * 2,
        scratch_shapes=[
            pltpu.VMEM((8, 256), jnp.int32),
            pltpu.VMEM((8, 256), jnp.int32),
            pltpu.SMEM((8, 256), jnp.int32),
            pltpu.VMEM((512, LANES), F32),
            pltpu.VMEM((512, LANES), F32),
            pltpu.VMEM((ROW_SLOTS, RANK, LANES), BF16),
            pltpu.VMEM((COLUMNS, RANK, LANES), BF16),
            pltpu.VMEM((COLUMNS, RANK, LANES), BF16),
            pltpu.VMEM((blocks + 1, HALF, LANES), BF16),
            pltpu.VMEM((blocks + 1, HALF, LANES), BF16),
            pltpu.VMEM(((blocks + 1) * HALF, LANES), F32),
            pltpu.VMEM((ROW_SLOTS, RANK, LANES), F32),
            pltpu.SemaphoreType.DMA,
        ],
        compiler_params=pltpu.CompilerParams(vmem_limit_bytes=40 * MIB),
        name="blocks",
    )(admissible, grams, leaf_factors, coupling)


def sum_kernel(reps, part, zero, one, two, parts, send, receive):
    leaf = lax.axis_index("leaf")
    me = lax.axis_index("rep")
    barrier = pltpu.get_barrier_semaphore()
    for step in range(1, reps):
        other = lax.rem(me + step, reps)
        pl.semaphore_signal(barrier, inc=1, device_id=(leaf, other), device_id_type=MESH)
    parts[me] = part[...].astype(BF16)
    pl.semaphore_wait(barrier, reps - 1)
    copies = []
    for step in range(1, reps):
        copy = pltpu.make_async_remote_copy(
            src_ref=parts.at[me], dst_ref=parts.at[me],
            send_sem=send.at[step - 1], recv_sem=receive.at[step - 1],
            device_id=(leaf, lax.rem(me + step, reps)), device_id_type=MESH,
        )
        copy.start()
        copies.append(copy)
    for copy in copies:
        copy.wait_recv()
    total = parts[0].astype(F32)
    for k in range(1, reps):
        total = total + parts[k].astype(F32)
    lines = part
    lines[...] = total
    for tile in range(HALF):
        span = slice(tile * LANES, (tile + 1) * LANES)
        zero[:, span] = lines[pl.ds(tile, CL_DEV, stride=HALF), :]
        one[:, span] = lines[pl.ds(tile + CL_DEV * HALF, CL_DEV // 2, stride=HALF), :]
        two[:, span] = lines[tile + (SLOTS - 1) * HALF : tile + (SLOTS - 1) * HALF + 1, :]
    for copy in copies:
        copy.wait_send()


def sum_kernel_outer(reps, part, zero, one, two, lines, parts, send, receive):
    lines[...] = part[...]
    sum_kernel(reps, lines, zero, one, two, parts, send, receive)


def sum_call(reps, part):
    vmem = pl.BlockSpec(memory_space=pltpu.VMEM)
    return pl.pallas_call(
        functools.partial(sum_kernel_outer, reps),
        out_shape=[jax.ShapeDtypeStruct((count, FLAT), F32) for count in (4, 2, 1)],
        in_specs=[vmem],
        out_specs=[vmem] * 3,
        scratch_shapes=[
            pltpu.VMEM(part.shape, F32),
            pltpu.VMEM((reps,) + part.shape, BF16),
            pltpu.SemaphoreType.DMA((reps - 1,)),
            pltpu.SemaphoreType.DMA((reps - 1,)),
        ],
        compiler_params=pltpu.CompilerParams(collective_id=1, has_side_effects=True),
        name="rep_sum",
    )(part)


def local(leaves, reps, bottom, zero, one, two, three, order, coupling, admissible):
    grams, leaf_factors = upsweep(leaves, order, bottom, zero, one, two, three)
    projected, part = blocks_call(admissible, grams, leaf_factors, coupling)
    weights = sum_call(reps, part)
    return projected, *weights


def solution(mesh):
    return jax.shard_map(
        functools.partial(local, mesh.shape["leaf"], mesh.shape["rep"]),
        mesh=mesh,
        in_specs=(
            P("leaf", None),
            P("leaf", None),
            P("leaf", None),
            P("leaf", None),
            P(),
            P("leaf", None),
            P(("leaf", "rep"), None),
            P(None, ("leaf", "rep")),
        ),
        out_specs=(P(("leaf", "rep"), None), P("leaf", None), P("leaf", None), P("leaf", None)),
        check_vma=False,
    )
```

time: 205 us -> 71.2 us (0.35)
  the two profiles are of different devices: /device:TPU:16 before, /device:TPU:4 now
where the time goes in v1:
time: 71.2 us; the launch traced here: 70.5 us
  Pallas kernels  57.9 us (81%)
  local copies, waits for them, and re-layouts  11.9 us (17%)
    pallas_call x1, Pallas kernels, blocks_call(): pl.pallas_call(functools.partial(blocks_kernel, blocks, pairs), out_shape...  32.3 us
    pallas_call x1, Pallas kernels, upsweep(): pl.pallas_call(functools.partial(upsweep_kernel, leaves, chunk), out_shap...  16.9 us
    unnamed x21, local copies, waits for them, and re-layouts  11.9 us
    pallas_call x1, Pallas kernels, sum_call(): pl.pallas_call(functools.partial(sum_kernel_outer, reps), out_shape=[jax....  8.72 us

profile of v1, /device:TPU:4, one launch (start us, length us, event | category | flops | bytes accessed | tf_op | source)
XLA Modules:
  0.0 70.5 jit_solution(5192528987594899365)
XLA Ops:
  0.6 0.0 copy-start.1
  0.6 1.2 %copy-done.1 = f32[64,4096]{1,0:T(8,128)S(1)} copy-done((f32[64,4096]{1,0:T(8,128)S(1)}, f32[64,4096]{1,0:T(8,128)}, u32[]{:S(2)}) %copy-start.1) | copy-done | bytes 1048600
  1.9 0.0 copy-start.3
  1.9 0.8 %copy-done.3 = f32[4,4096]{1,0:T(4,128)S(1)} copy-done((f32[4,4096]{1,0:T(4,128)S(1)}, f32[4,4096]{1,0:T(4,128)}, u32[]{:S(2)}) %copy-start.3) | copy-done | bytes 65560
  2.7 0.0 copy-start.4
  2.7 0.8 %copy-done.4 = f32[4,4096]{1,0:T(4,128)S(1)} copy-done((f32[4,4096]{1,0:T(4,128)S(1)}, f32[4,4096]{1,0:T(4,128)}, u32[]{:S(2)}) %copy-start.4) | copy-done | bytes 65560
  3.5 0.0 copy-start.5
  3.5 0.8 %copy-done.5 = f32[2,4096]{1,0:T(2,128)S(1)} copy-done((f32[2,4096]{1,0:T(2,128)S(1)}, f32[2,4096]{1,0:T(2,128)}, u32[]{:S(2)}) %copy-start.5) | copy-done | bytes 32792
  4.3 0.0 copy-start.6
  4.3 0.7 %copy-done.6 = f32[1,4096]{1,0:T(1,128)S(1)} copy-done((f32[1,4096]{1,0:T(1,128)S(1)}, f32[1,4096]{1,0:T(1,128)}, u32[]{:S(2)}) %copy-start.6) | copy-done | bytes 16408
  5.0 0.0 copy-start.8
  5.0 0.7 copy-done.8
  5.7 16.9 %upsweep.1 = (f32[512,128]{1,0:T(8,128)S(1)}, bf16[384,128]{1,0:T(8,128)(2,1)S(1)}) custom-call(s32[1,4]{1,0:T(1,128)S(1)} %copy-done.8, f32[4,4096]{1,0:T(4,128)S(1)} %copy-done.3, f32[4,4096]{1,0:T(4,128)S(1)} %copy-done.4, f32[2,4096]{1,0:T(2,128)S(1)} %copy-done.5, f32[1,4096]{1,0:T(1,128)S(1)} %copy-done.6, f32[64,4096]{1,0:T(8,128)S(1)} %copy-done.1), custom_call_target="tpu_custom_call" | custom-call | tf_op jit(solution)/shard_map/upsweep/pallas_call | solution.py:173
  22.6 0.0 copy-start
  22.6 1.4 %copy-done = bf16[192,4096]{1,0:T(8,128)(2,1)S(1)} copy-done((bf16[192,4096]{1,0:T(8,128)(2,1)S(1)}, bf16[192,4096]{1,0:T(8,128)(2,1)}, u32[]{:S(2)}) %copy-start) | copy-done | bytes 1572888
  24.0 0.0 copy-start.7
  24.0 0.7 copy-done.7
  24.7 32.3 %blocks.1 = (bf16[192,4096]{1,0:T(8,128)(2,1)}, f32[224,128]{1,0:T(8,128)S(1)}) custom-call(s32[3,192]{1,0:T(4,128)S(1)} %copy-done.7, f32[512,128]{1,0:T(8,128)S(1)} %get-tuple-element.11.grams, bf16[384,128]{1,0:T(8,128)(2,1)S(1)} %get-tuple-element.12.leaf_factors, bf16[192,4096]{1,0:T(8,128)(2,1)S(1)} %copy-done), custom_call_target="tpu_custom_call" | custom-call | tf_op jit(solution)/shard_map/blocks/pallas_call | solution.py:416
  57.0 0.0 copy-start.2
  57.0 0.6 copy-done.2
  57.6 8.7 %rep_sum.1 = (f32[4,4096]{1,0:T(4,128)}, f32[2,4096]{1,0:T(2,128)}, f32[1,4096]{1,0:T(1,128)}) custom-call(f32[224,128]{1,0:T(8,128)} %copy-done.2), custom_call_target="tpu_custom_call" | custom-call | tf_op jit(solution)/shard_map/rep_sum/pallas_call | solution.py:485
  66.3 1.5 %copy.15 = f32[4,4096]{1,0:T(4,128)} copy(f32[4,4096]{1,0:T(4,128)} %get-tuple-element.23) | data formatting | bytes 131072
  67.8 1.4 %copy.16 = f32[2,4096]{1,0:T(2,128)} copy(f32[2,4096]{1,0:T(2,128)} %get-tuple-element.24) | data formatting | bytes 65536
  69.2 1.3 %copy.17 = f32[1,4096]{1,0:T(1,128)} copy(f32[1,4096]{1,0:T(1,128)} %get-tuple-element.25) | data formatting | bytes 32768
Async XLA Ops:
  0.6 1.2 %copy-start.1 = (f32[64,4096]{1,0:T(8,128)S(1)}, f32[64,4096]{1,0:T(8,128)}, u32[]{:S(2)}) copy-start(f32[64,4096]{1,0:T(8,128)} %three.1) | copy-start | bytes 3145732
  1.9 0.8 %copy-start.3 = (f32[4,4096]{1,0:T(4,128)S(1)}, f32[4,4096]{1,0:T(4,128)}, u32[]{:S(2)}) copy-start(f32[4,4096]{1,0:T(4,128)} %bottom.1) | copy-start | bytes 196612
  2.7 0.8 %copy-start.4 = (f32[4,4096]{1,0:T(4,128)S(1)}, f32[4,4096]{1,0:T(4,128)}, u32[]{:S(2)}) copy-start(f32[4,4096]{1,0:T(4,128)} %zero.1) | copy-start | bytes 196612
  3.5 0.8 %copy-start.5 = (f32[2,4096]{1,0:T(2,128)S(1)}, f32[2,4096]{1,0:T(2,128)}, u32[]{:S(2)}) copy-start(f32[2,4096]{1,0:T(2,128)} %one.1) | copy-start | bytes 98308
  4.3 0.7 %copy-start.6 = (f32[1,4096]{1,0:T(1,128)S(1)}, f32[1,4096]{1,0:T(1,128)}, u32[]{:S(2)}) copy-start(f32[1,4096]{1,0:T(1,128)} %two.1) | copy-start | bytes 49156
  5.0 0.7 copy-start.8
  22.6 1.4 %copy-start = (bf16[192,4096]{1,0:T(8,128)(2,1)S(1)}, bf16[192,4096]{1,0:T(8,128)(2,1)}, u32[]{:S(2)}) copy-start(bf16[192,4096]{1,0:T(8,128)(2,1)} %coupling.1) | copy-start | bytes 4718596
  24.0 0.7 copy-start.7
  57.0 0.6 copy-start.2

commit v2 on v1

--- a/solution.py
+++ b/solution.py
@@ -20,6 +20,8 @@
 F32 = jnp.float32
 BF16 = jnp.bfloat16
 EXACT = lax.Precision.HIGHEST
+WIDE = 256
+BATCH = 25
 MIB = 1024 * 1024
 
 
@@ -71,25 +73,74 @@
     return jnp.concatenate([x[:, :RANK], x[:, RANK:]], axis=0)
 
 
+def visit_order(admissible, leaf, padded_in):
+    padded_in[...] = jnp.full(padded_in.shape, -1, jnp.int32)
+    padded_in[0:3, 0 : admissible.shape[1]] = admissible[...]
+    level = padded_in[0:1, :]
+    row = padded_in[1:2, :]
+    column = padded_in[2:3, :]
+    low = level <= 2
+    base = jnp.where(level == 0, 0, jnp.where(level == 1, CL_DEV, CL_DEV + CL_DEV // 2))
+    shift = jnp.where(level == 0, 2, jnp.where(level == 1, 1, 0))
+    held = jnp.left_shift(1, shift) - 1
+    slot = jnp.where(low, base + jnp.bitwise_and(row, held), level + (SLOTS - 3))
+    slot = jnp.where(level < 0, -1, slot)
+    side = jnp.clip(jnp.right_shift(column, shift) - leaf + 1, 0, 2)
+    place = jnp.where(
+        low, side * SLOTS + base + jnp.bitwise_and(column, held), 3 * SLOTS + level - 3
+    )
+    member = lax.broadcasted_iota(jnp.int32, (16, WIDE), 0) == slot
+    ahead = lax.broadcasted_iota(jnp.int32, (WIDE, WIDE), 0) <= lax.broadcasted_iota(
+        jnp.int32, (WIDE, WIDE), 1
+    )
+    member_f = jnp.where(member, 1.0, 0.0).astype(F32)
+    rank = jnp.dot(member_f.astype(BF16), jnp.where(ahead, 1.0, 0.0).astype(BF16), preferred_element_type=F32)
+    count = jnp.sum(member_f, axis=1, keepdims=True)
+    even = jnp.floor((count + 1.0) * 0.5) * 2.0
+    even = jnp.broadcast_to(even, (16, WIDE)).astype(BF16)
+    below = lax.broadcasted_iota(jnp.int32, (16, 16), 1) < lax.broadcasted_iota(jnp.int32, (16, 16), 0)
+    begin = jnp.dot(jnp.where(below, 1.0, 0.0).astype(BF16), even, preferred_element_type=F32)
+    at = jnp.sum(jnp.where(member, begin + rank - 1.0, 0.0), axis=0, keepdims=True)
+    at = jnp.where(slot < 0, -1.0, at).astype(jnp.int32)
+    chosen = lax.broadcasted_iota(jnp.int32, (WIDE, WIDE), 0) == at
+    line = lax.broadcasted_iota(jnp.int32, (8, WIDE), 0)
+    number = lax.broadcasted_iota(jnp.int32, (8, WIDE), 1) + 1
+    values = jnp.where(line == 0, number, jnp.where(line == 1, place, jnp.where(line == 2, slot, 0)))
+    return lax.dot_general(
+        values.astype(F32).astype(BF16), jnp.where(chosen, 1.0, 0.0).astype(BF16),
+        (((1,), (1,)), ((), ())), preferred_element_type=F32,
+    ).astype(jnp.int32)
+
+
 def upsweep_kernel(
     leaves, chunk,
-    order, bottom, zero, one, two, three,
-    grams_out, factors_out,
-    lines, lines_three, flat_three, page, kids, factors, pairs, tops, images,
-    three_sem, send, receive,
+    order_in, bottom_in, zero_in, one_in, two_in, three_in,
+    grams_to, factors_to,
+    order, bottom, zero, one, two, three, grams_out,
+    lines, lines_three, page, kids, factors, pairs, tops,
+    fetched, stored, send, receive,
 ):
     me = lax.axis_index("leaf")
     rep = lax.axis_index("rep")
     left = lax.rem(me + leaves - 1, leaves)
     right = lax.rem(me + 1, leaves)
     others = [flipped(me, bits) for bits in range(1, GROUP)]
+    start = pl.multiple_of(me // 2 // chunk * chunk, chunk)
+    sources = [
+        bottom_in, zero_in, order_in, one_in, two_in, three_in.at[pl.ds(start, chunk)],
+    ]
+    targets = [bottom, zero, order, one, two, three]
+    fetches = [
+        pltpu.make_async_copy(source, target, fetched.at[k])
+        for k, (source, target) in enumerate(zip(sources, targets))
+    ]
+    for fetch in fetches:
+        fetch.start()
     barrier = pltpu.get_barrier_semaphore()
     for other in [left, right] + others:
         pl.semaphore_signal(barrier, inc=1, device_id=(other, rep), device_id_type=MESH)
-    start = pl.multiple_of(me // 2 // chunk * chunk, chunk)
-    fetch = pltpu.make_async_copy(three.at[pl.ds(start, chunk)], flat_three, three_sem)
-    fetch.start()
-
+    for fetch in fetches[:5]:
+        fetch.wait()
     tiles_of(bottom, CL_DEV, lines)
     bottoms = [packed(lines, c) for c in range(CL_DEV)]
     leaf_pairs = [natural_pair(bottoms[c], bottoms[c + 1], page) for c in (0, 2)]
@@ -136,8 +187,8 @@
     push(factors.at[1], factors.at[2], left)
     push(factors.at[1], factors.at[0], right)
 
-    fetch.wait()
-    tiles_of(flat_three, chunk, lines_three)
+    fetches[5].wait()
+    tiles_of(three, chunk, lines_three)
     place = lax.rem(me // 2, chunk)
     threes = []
     for u in range(GROUP // 2):
@@ -153,47 +204,58 @@
     level_four = [lifted[0] + lifted[1], lifted[2] + lifted[3]]
     for copy in copies[GROUP - 1 :]:
         copy.wait_recv()
+    stores = [pltpu.make_async_copy(factors, factors_to, stored.at[0])]
+    stores[0].start()
     for side in range(3):
         grams_out[side * RANK : (side + 1) * RANK, :] = pairs[side, :RANK, :]
-        factors_out[side * LANES : (side + 1) * LANES, :] = factors[side]
     side_two = [unpack(pairs[side, RANK:, :]) for side in range(3)]
     rest = side_two + [level_three[0], level_three[1], level_four[0], level_four[1], level_four[1]]
     for k in range(4):
         at = (3 + k) * RANK
         grams_out[at : at + RANK, :] = jnp.concatenate([rest[2 * k], rest[2 * k + 1]], axis=1)
     grams_out[7 * RANK :, :] = pairs[1, :RANK, :]
+    stores.append(pltpu.make_async_copy(grams_out, grams_to, stored.at[1]))
+    stores[1].start()
+    for store in stores:
+        store.wait()
     for copy in copies:
         copy.wait_send()
 
 
 def upsweep(leaves, order, bottom, zero, one, two, three):
     chunk = min(8, three.shape[0])
-    vmem = pl.BlockSpec(memory_space=pltpu.VMEM)
+    hbm = pl.BlockSpec(memory_space=pltpu.HBM)
     count = GROUP + 3
     return pl.pallas_call(
         functools.partial(upsweep_kernel, leaves, chunk),
         out_shape=[
             jax.ShapeDtypeStruct((8 * RANK, LANES), F32),
-            jax.ShapeDtypeStruct((3 * LANES, LANES), BF16),
+            jax.ShapeDtypeStruct((3, LANES, LANES), BF16),
         ],
-        in_specs=[pl.BlockSpec(memory_space=pltpu.SMEM)] + [vmem] * 4 + [pl.BlockSpec(memory_space=pl.ANY)],
-        out_specs=[vmem, vmem],
+        in_specs=[hbm] * 6,
+        out_specs=[hbm] * 2,
         scratch_shapes=[
+            pltpu.SMEM(order.shape, jnp.int32),
+            pltpu.VMEM(bottom.shape, F32),
+            pltpu.VMEM(zero.shape, F32),
+            pltpu.VMEM(one.shape, F32),
+            pltpu.VMEM(two.shape, F32),
+            pltpu.VMEM((chunk, FLAT), F32),
+            pltpu.VMEM((8 * RANK, LANES), F32),
             pltpu.VMEM((HALF * 8, LANES), F32),
             pltpu.VMEM((HALF * 8, LANES), F32),
-            pltpu.VMEM((chunk, FLAT), F32),
             pltpu.VMEM((RANK, LANES), F32),
             pltpu.VMEM((CL_DEV, RANK, RANK), F32),
             pltpu.VMEM((3, LANES, LANES), BF16),
             pltpu.VMEM((3, RANK + HALF, LANES), F32),
             pltpu.VMEM((GROUP, HALF, LANES), F32),
-            pltpu.VMEM((8, LANES), F32),
-            pltpu.SemaphoreType.DMA,
+            pltpu.SemaphoreType.DMA((6,)),
+            pltpu.SemaphoreType.DMA((2,)),
             pltpu.SemaphoreType.DMA((count,)),
             pltpu.SemaphoreType.DMA((count,)),
         ],
         compiler_params=pltpu.CompilerParams(
-            collective_id=0, has_side_effects=True, vmem_limit_bytes=32 * MIB
+            collective_id=0, has_side_effects=True, vmem_limit_bytes=60 * MIB
         ),
         name="upsweep",
     )(order, bottom, zero, one, two, three)
@@ -232,64 +294,40 @@
     return result
 
 
-def visit_order(admissible, leaf, padded_in):
-    wide = 256
-    padded_in[...] = jnp.full(padded_in.shape, -1, jnp.int32)
-    padded_in[0:3, 0 : admissible.shape[1]] = admissible[...]
-    level = padded_in[0:1, :]
-    row = padded_in[1:2, :]
-    column = padded_in[2:3, :]
-    low = level <= 2
-    base = jnp.where(level == 0, 0, jnp.where(level == 1, CL_DEV, CL_DEV + CL_DEV // 2))
-    shift = jnp.where(level == 0, 2, jnp.where(level == 1, 1, 0))
-    held = jnp.left_shift(1, shift) - 1
-    slot = jnp.where(low, base + jnp.bitwise_and(row, held), level + (SLOTS - 3))
-    slot = jnp.where(level < 0, -1, slot)
-    side = jnp.clip(jnp.right_shift(column, shift) - leaf + 1, 0, 2)
-    place = jnp.where(
-        low, side * SLOTS + base + jnp.bitwise_and(column, held), 3 * SLOTS + level - 3
-    )
-    member = lax.broadcasted_iota(jnp.int32, (16, wide), 0) == slot
-    ahead = lax.broadcasted_iota(jnp.int32, (wide, wide), 0) <= lax.broadcasted_iota(
-        jnp.int32, (wide, wide), 1
-    )
-    member_f = jnp.where(member, 1.0, 0.0).astype(F32)
-    rank = jnp.dot(member_f.astype(BF16), jnp.where(ahead, 1.0, 0.0).astype(BF16), preferred_element_type=F32)
-    count = jnp.sum(member_f, axis=1, keepdims=True)
-    even = jnp.floor((count + 1.0) * 0.5) * 2.0
-    even = jnp.broadcast_to(even, (16, wide)).astype(BF16)
-    below = lax.broadcasted_iota(jnp.int32, (16, 16), 1) < lax.broadcasted_iota(jnp.int32, (16, 16), 0)
-    begin = jnp.dot(jnp.where(below, 1.0, 0.0).astype(BF16), even, preferred_element_type=F32)
-    at = jnp.sum(jnp.where(member, begin + rank - 1.0, 0.0), axis=0, keepdims=True)
-    at = jnp.where(slot < 0, -1.0, at).astype(jnp.int32)
-    chosen = lax.broadcasted_iota(jnp.int32, (wide, wide), 0) == at
-    line = lax.broadcasted_iota(jnp.int32, (8, wide), 0)
-    number = lax.broadcasted_iota(jnp.int32, (8, wide), 1) + 1
-    values = jnp.where(line == 0, number, jnp.where(line == 1, place, jnp.where(line == 2, slot, 0)))
-    return lax.dot_general(
-        values.astype(F32).astype(BF16), jnp.where(chosen, 1.0, 0.0).astype(BF16),
-        (((1,), (1,)), ((), ())), preferred_element_type=F32,
-    ).astype(jnp.int32)
-
-
 def blocks_kernel(
     blocks, pairs,
-    admissible, grams, leaf_factors, coupling,
-    projected, weights_out,
-    padded_in, order_v, order, lines, upper, row_table, column_left, column_right,
-    own, turned, results, totals, order_sem,
+    admissible_in, grams_in, factors_in, coupling_in,
+    projected_to, weights_to,
+    admissible, grams, leaf_factors, coupling, projected, weights_out,
+    padded_in, visits_v, order, lines, upper, row_table, column_left, column_right,
+    own, turned, results, totals, fetched, stored, order_sem,
 ):
     leaf = lax.axis_index("leaf")
+    fetches = [
+        pltpu.make_async_copy(source, target, fetched.at[k])
+        for k, (source, target) in enumerate((
+            (admissible_in, admissible), (grams_in, grams),
+            (factors_in, leaf_factors), (coupling_in, coupling),
+        ))
+    ]
+    for fetch in fetches:
+        fetch.start()
     side = lanes_left(HALF)
     side_full = lanes_left(RANK)
     lane = lax.broadcasted_iota(jnp.int32, (RANK, LANES), 1)
     inner = jnp.where(lane < RANK, lane, lane - RANK)
     spread = jnp.where(inner < HALF, 2 * inner, 2 * inner - (RANK - 1)) + (lane - inner)
 
-    order_v[...] = visit_order(admissible, leaf, padded_in)
-    to_scalar = pltpu.make_async_copy(order_v, order, order_sem)
+    fetches[0].wait()
+    visits_v[...] = visit_order(admissible, leaf, padded_in)
+    to_scalar = pltpu.make_async_copy(visits_v, order, order_sem)
     to_scalar.start()
-
+    fetches[1].wait()
+    rows = factorize([grams[pl.ds(i, 8, stride=RANK), :] for i in range(RANK)])
+    for i in range(RANK):
+        upper[i * 8 : (i + 1) * 8, :] = rows[i]
+
+    fetches[3].wait()
     own[0] = jnp.zeros((HALF, LANES), BF16)
     turned[0] = jnp.zeros((HALF, LANES), BF16)
 
@@ -308,9 +346,7 @@
 
     lax.fori_loop(0, blocks // 16, lay, 0)
 
-    rows = factorize([grams[pl.ds(i, 8, stride=RANK), :] for i in range(RANK)])
-    for i in range(RANK):
-        upper[i * 8 : (i + 1) * 8, :] = rows[i]
+    fetches[2].wait()
 
     def put_column(where, left, right):
         column_left[where] = left.astype(BF16)
@@ -334,8 +370,8 @@
             row_table[names[1]] = swap(x).astype(BF16)
 
     for near in range(3):
-        first = leaf_factors[near * LANES : near * LANES + RANK, :].astype(F32)
-        second = leaf_factors[near * LANES + RANK : (near + 1) * LANES, :].astype(F32)
+        first = leaf_factors[near, :RANK, :].astype(F32)
+        second = leaf_factors[near, RANK:, :].astype(F32)
         put_columns(first, second, [near * SLOTS + c for c in (0, 1, 2, 3)])
         if near == 1:
             for k, x in enumerate((first, second)):
@@ -360,36 +396,53 @@
     totals[...] = jnp.zeros(totals.shape, F32)
     to_scalar.wait()
 
-    def visit(pair):
-        a, b = order[0, 2 * pair], order[0, 2 * pair + 1]
-        slot = order[2, 2 * pair]
-        both = jnp.concatenate(
-            [jnp.where(side, own[a], turned[b]), jnp.where(side, turned[a], own[b])], axis=0
-        )
-        half = jnp.dot(row_table[slot][:, :RANK], both, preferred_element_type=F32).astype(BF16)
-        columns = jnp.concatenate(
-            [column_left[order[1, 2 * pair]], column_right[order[1, 2 * pair + 1]]], axis=0
-        )
-        result = jnp.dot(half, columns, preferred_element_type=F32)
-        rounded = result.astype(BF16)
-        totals[slot, :, :RANK] += lax.dot_general(
-            rounded, rounded, (((1,), (1,)), ((), ())), preferred_element_type=F32
-        )
-        top, bottom = result[:HALF], result[HALF:]
-        results[pl.ds(pl.multiple_of(a * HALF, HALF), HALF), :] = jnp.where(side, top, swap(bottom))
-        results[pl.ds(pl.multiple_of(b * HALF, HALF), HALF), :] = jnp.where(side, swap(top), bottom)
-
     def visits(step, carry):
-        for k in range(4):
-            visit(step * 4 + k)
+        places = [step * BATCH + k for k in range(BATCH)]
+        halves = []
+        for pair in places:
+            a, b = order[0, 2 * pair], order[0, 2 * pair + 1]
+            both = jnp.concatenate(
+                [jnp.where(side, own[a], turned[b]), jnp.where(side, turned[a], own[b])], axis=0
+            )
+            slot = order[2, 2 * pair]
+            halves.append(
+                jnp.dot(row_table[slot][:, :RANK], both, preferred_element_type=F32).astype(BF16)
+            )
+        products = []
+        for pair, half in zip(places, halves):
+            columns = jnp.concatenate(
+                [column_left[order[1, 2 * pair]], column_right[order[1, 2 * pair + 1]]], axis=0
+            )
+            products.append(jnp.dot(half, columns, preferred_element_type=F32))
+        terms = []
+        for product in products:
+            rounded = product.astype(BF16)
+            terms.append(lax.dot_general(
+                rounded, rounded, (((1,), (1,)), ((), ())), preferred_element_type=F32
+            ))
+        for pair, result in zip(places, products):
+            a, b = order[0, 2 * pair], order[0, 2 * pair + 1]
+            top, bottom = result[:HALF], result[HALF:]
+            results[pl.ds(pl.multiple_of(a * HALF, HALF), HALF), :] = jnp.where(side, top, swap(bottom))
+            results[pl.ds(pl.multiple_of(b * HALF, HALF), HALF), :] = jnp.where(side, swap(top), bottom)
+        for pair, term in zip(places, terms):
+            slot = order[2, 2 * pair]
+            totals[slot, :, :RANK] += term
         return carry
 
-    lax.fori_loop(0, pairs // 4, visits, 0)
+    lax.fori_loop(0, pairs // BATCH, visits, 0)
 
     gather = jnp.where(inner % 2 == 0, inner // 2, HALF + inner // 2)
     for s in range(SLOTS):
         x = picked(totals[s], gather)
         weights_out[s * HALF : (s + 1) * HALF, :] = jnp.where(side, x[:HALF], x[HALF:]) * (1.0 / RANK)
+    groups = blocks // 16
+    weights_store = pltpu.make_async_copy(weights_out, weights_to, stored.at[groups])
+    weights_store.start()
+
+    def store_of(group):
+        span = pl.ds(pl.multiple_of(group * 16, 16), 16)
+        return pltpu.make_async_copy(projected.at[span], projected_to.at[span], stored.at[group])
 
     def write(group, carry):
         first = pl.multiple_of(group * 16, 16)
@@ -403,28 +456,38 @@
                 axis=0,
             )
             projected[pl.ds(first, 16), tile * LANES : (tile + 1) * LANES] = x.astype(BF16)
+        store_of(group).start()
         return carry
 
-    lax.fori_loop(0, blocks // 16, write, 0)
+    lax.fori_loop(0, groups, write, 0)
+    weights_store.wait()
+    for group in range(groups):
+        store_of(group).wait()
 
 
 def blocks_call(admissible, grams, leaf_factors, coupling):
     blocks = coupling.shape[0]
     pairs = -(-(blocks + ROW_SLOTS) // 2)
-    pairs = -(-pairs // 4) * 4
-    vmem = pl.BlockSpec(memory_space=pltpu.VMEM)
+    pairs = -(-pairs // BATCH) * BATCH
+    hbm = pl.BlockSpec(memory_space=pltpu.HBM)
     return pl.pallas_call(
         functools.partial(blocks_kernel, blocks, pairs),
         out_shape=[
             jax.ShapeDtypeStruct((blocks, FLAT), BF16),
             jax.ShapeDtypeStruct((SLOTS * HALF, LANES), F32),
         ],
-        in_specs=[vmem] * 4,
-        out_specs=[vmem] * 2,
+        in_specs=[hbm] * 4,
+        out_specs=[hbm] * 2,
         scratch_shapes=[
-            pltpu.VMEM((8, 256), jnp.int32),
-            pltpu.VMEM((8, 256), jnp.int32),
-            pltpu.SMEM((8, 256), jnp.int32),
+            pltpu.VMEM(admissible.shape, jnp.int32),
+            pltpu.VMEM(grams.shape, F32),
+            pltpu.VMEM(leaf_factors.shape, BF16),
+            pltpu.VMEM(coupling.shape, BF16),
+            pltpu.VMEM(coupling.shape, BF16),
+            pltpu.VMEM((SLOTS * HALF, LANES), F32),
+            pltpu.VMEM((8, WIDE), jnp.int32),
+            pltpu.VMEM((8, WIDE), jnp.int32),
+            pltpu.SMEM((8, WIDE), jnp.int32),
             pltpu.VMEM((512, LANES), F32),
             pltpu.VMEM((512, LANES), F32),
             pltpu.VMEM((ROW_SLOTS, RANK, LANES), BF16),
@@ -434,14 +497,16 @@
             pltpu.VMEM((blocks + 1, HALF, LANES), BF16),
             pltpu.VMEM(((blocks + 1) * HALF, LANES), F32),
             pltpu.VMEM((ROW_SLOTS, RANK, LANES), F32),
+            pltpu.SemaphoreType.DMA((4,)),
+            pltpu.SemaphoreType.DMA((blocks // 16 + 1,)),
             pltpu.SemaphoreType.DMA,
         ],
-        compiler_params=pltpu.CompilerParams(vmem_limit_bytes=40 * MIB),
+        compiler_params=pltpu.CompilerParams(vmem_limit_bytes=60 * MIB),
         name="blocks",
     )(admissible, grams, leaf_factors, coupling)
 
 
-def sum_kernel(reps, part, zero, one, two, parts, send, receive):
+def sum_kernel(reps, part, total, parts, send, receive):
     leaf = lax.axis_index("leaf")
     me = lax.axis_index("rep")
     barrier = pltpu.get_barrier_semaphore()
@@ -461,48 +526,65 @@
         copies.append(copy)
     for copy in copies:
         copy.wait_recv()
-    total = parts[0].astype(F32)
+    added = parts[0].astype(F32)
     for k in range(1, reps):
-        total = total + parts[k].astype(F32)
-    lines = part
-    lines[...] = total
-    for tile in range(HALF):
-        span = slice(tile * LANES, (tile + 1) * LANES)
-        zero[:, span] = lines[pl.ds(tile, CL_DEV, stride=HALF), :]
-        one[:, span] = lines[pl.ds(tile + CL_DEV * HALF, CL_DEV // 2, stride=HALF), :]
-        two[:, span] = lines[tile + (SLOTS - 1) * HALF : tile + (SLOTS - 1) * HALF + 1, :]
+        added = added + parts[k].astype(F32)
+    total[...] = added
     for copy in copies:
         copy.wait_send()
 
 
-def sum_kernel_outer(reps, part, zero, one, two, lines, parts, send, receive):
-    lines[...] = part[...]
-    sum_kernel(reps, lines, zero, one, two, parts, send, receive)
-
-
 def sum_call(reps, part):
-    vmem = pl.BlockSpec(memory_space=pltpu.VMEM)
     return pl.pallas_call(
-        functools.partial(sum_kernel_outer, reps),
-        out_shape=[jax.ShapeDtypeStruct((count, FLAT), F32) for count in (4, 2, 1)],
-        in_specs=[vmem],
-        out_specs=[vmem] * 3,
+        functools.partial(sum_kernel, reps),
+        out_shape=jax.ShapeDtypeStruct(part.shape, F32),
+        in_specs=[pl.BlockSpec(memory_space=pltpu.VMEM)],
+        out_specs=pl.BlockSpec(memory_space=pltpu.VMEM),
         scratch_shapes=[
-            pltpu.VMEM(part.shape, F32),
             pltpu.VMEM((reps,) + part.shape, BF16),
             pltpu.SemaphoreType.DMA((reps - 1,)),
             pltpu.SemaphoreType.DMA((reps - 1,)),
         ],
-        compiler_params=pltpu.CompilerParams(collective_id=1, has_side_effects=True),
+        compiler_params=pltpu.CompilerParams(
+            collective_id=1, has_side_effects=True, vmem_limit_bytes=16 * MIB
+        ),
         name="rep_sum",
     )(part)
+
+
+def deliver_kernel(total, zero, one, two, zero_v, one_v, two_v, sems):
+    for tile in range(HALF):
+        span = slice(tile * LANES, (tile + 1) * LANES)
+        zero_v[:, span] = total[pl.ds(tile, CL_DEV, stride=HALF), :]
+        one_v[:, span] = total[pl.ds(tile + CL_DEV * HALF, CL_DEV // 2, stride=HALF), :]
+        at = tile + (SLOTS - 1) * HALF
+        two_v[:, span] = total[at : at + 1, :]
+    copies = [
+        pltpu.make_async_copy(source, target, sems.at[k])
+        for k, (source, target) in enumerate(((zero_v, zero), (one_v, one), (two_v, two)))
+    ]
+    for copy in copies:
+        copy.start()
+    for copy in copies:
+        copy.wait()
+
+
+def deliver_call(total):
+    small = [(count, FLAT) for count in (CL_DEV, CL_DEV // 2, 1)]
+    return pl.pallas_call(
+        deliver_kernel,
+        out_shape=[jax.ShapeDtypeStruct(shape, F32) for shape in small],
+        in_specs=[pl.BlockSpec(memory_space=pltpu.VMEM)],
+        out_specs=[pl.BlockSpec(memory_space=pltpu.HBM)] * 3,
+        scratch_shapes=[pltpu.VMEM(shape, F32) for shape in small] + [pltpu.SemaphoreType.DMA((3,))],
+        name="deliver",
+    )(total)
 
 
 def local(leaves, reps, bottom, zero, one, two, three, order, coupling, admissible):
     grams, leaf_factors = upsweep(leaves, order, bottom, zero, one, two, three)
     projected, part = blocks_call(admissible, grams, leaf_factors, coupling)
-    weights = sum_call(reps, part)
-    return projected, *weights
+    return projected, *deliver_call(sum_call(reps, part))
 
 
 def solution(mesh):

time: 71.2 us -> 43.9 us (0.62)
  Pallas kernels: 57.9 us -> 41.5 us
  local copies, waits for them, and re-layouts: 11.9 us -> 1.52 us
    pallas_call x1, Pallas kernels: 32.3 us -> 15 us  [blocks_call(): pl.pallas_call(functools.partial(blocks_kernel, blocks, pairs), out_shape...]
    unnamed x21 -> x4, local copies, waits for them, and re-layouts: 11.9 us -> 1.52 us
    pallas_call x1, Pallas kernels: 16.9 us -> 17.7 us  [upsweep(): pl.pallas_call(functools.partial(upsweep_kernel, leaves, chunk), out_shap...]
    pallas_call x1 -> x2, Pallas kernels: 8.72 us -> 8.72 us  [the longest x1 7.1 us: sum_call(): pl.pallas_call(functools.partial(sum_kernel, reps), out_shape=jax.ShapeDt...]
where the time goes in v2:
time: 43.9 us; the launch traced here: 43.7 us
  Pallas kernels  41.5 us (95%)
  local copies, waits for them, and re-layouts  1.52 us (3%)
  between operations  0.67 us (2%)
    pallas_call x1, Pallas kernels, upsweep(): pl.pallas_call(functools.partial(upsweep_kernel, leaves, chunk), out_shap...  17.7 us
    pallas_call x1, Pallas kernels, blocks_call(): pl.pallas_call(functools.partial(blocks_kernel, blocks, pairs), out_shape...  15 us
    pallas_call x1, Pallas kernels, sum_call(): pl.pallas_call(functools.partial(sum_kernel, reps), out_shape=jax.ShapeDt...  7.1 us
    pallas_call x1, Pallas kernels, deliver_call(): pl.pallas_call(deliver_kernel, out_shape=[jax.ShapeDtypeStruct(shape, F32...  1.63 us
    unnamed x4, local copies, waits for them, and re-layouts  1.52 us

profile of v2, /device:TPU:4, one launch (start us, length us, event | category | flops | bytes accessed | tf_op | source)
XLA Modules:
  0.0 43.7 jit_solution(2658321925847507704)
XLA Ops:
  0.6 17.7 %upsweep.1 = (f32[512,128]{1,0:T(8,128)}, bf16[3,128,128]{2,1,0:T(8,128)(2,1)}) custom-call(s32[1,4]{1,0:T(1,128)} %order_in.1, f32[4,4096]{1,0:T(4,128)} %bottom_in.1, f32[4,4096]{1,0:T(4,128)} %zero_in.1, f32[2,4096]{1,0:T(2,128)} %one_in.1, f32[1,4096]{1,0:T(1,128)} %two_in.1, f32[64,4096]{1,0:T(8,128)} %three_in.1), custom_call_target="tpu_custom_call" | custom-call | tf_op jit(solution)/shard_map/upsweep/pallas_call | solution.py:229
  18.4 15.0 %blocks.1 = (bf16[192,4096]{1,0:T(8,128)(2,1)}, f32[224,128]{1,0:T(8,128)}) custom-call(s32[3,192]{1,0:T(4,128)} %admissible_in.1, f32[512,128]{1,0:T(8,128)} %get-tuple-element.11.grams_in, bf16[3,128,128]{2,1,0:T(8,128)(2,1)} %get-tuple-element.12.factors_in, bf16[192,4096]{1,0:T(8,128)(2,1)} %coupling_in.1), custom_call_target="tpu_custom_call" | custom-call | tf_op jit(solution)/shard_map/blocks/pallas_call | solution.py:473
  33.4 0.0 copy-start.1
  33.4 0.9 %copy-done.1 = f32[224,128]{1,0:T(8,128)S(1)} copy-done((f32[224,128]{1,0:T(8,128)S(1)}, f32[224,128]{1,0:T(8,128)}, u32[]{:S(2)}) %copy-start.1) | copy-done | bytes 114712
  34.3 7.1 %rep_sum.1.total = f32[224,128]{1,0:T(8,128)S(1)} custom-call(f32[224,128]{1,0:T(8,128)S(1)} %copy-done.1), custom_call_target="tpu_custom_call" | custom-call | tf_op jit(solution)/shard_map/rep_sum/pallas_call | solution.py:538
  41.4 0.0 copy-start
  41.4 0.6 %copy-done = f32[224,128]{1,0:T(8,128)} copy-done((f32[224,128]{1,0:T(8,128)}, f32[224,128]{1,0:T(8,128)S(1)}, u32[]{:S(2)}) %copy-start) | copy-done | bytes 114712
  42.0 1.6 %deliver.1 = (f32[4,4096]{1,0:T(4,128)}, f32[2,4096]{1,0:T(2,128)}, f32[1,4096]{1,0:T(1,128)}) custom-call(f32[224,128]{1,0:T(8,128)} %copy-done), custom_call_target="tpu_custom_call" | custom-call | tf_op jit(solution)/shard_map/deliver/pallas_call | solution.py:574
Async XLA Ops:
  33.4 0.9 %copy-start.1 = (f32[224,128]{1,0:T(8,128)S(1)}, f32[224,128]{1,0:T(8,128)}, u32[]{:S(2)}) copy-start(f32[224,128]{1,0:T(8,128)} %get-tuple-element.14.part) | copy-start | bytes 344068
  41.4 0.6 %copy-start = (f32[224,128]{1,0:T(8,128)}, f32[224,128]{1,0:T(8,128)S(1)}, u32[]{:S(2)}) copy-start(f32[224,128]{1,0:T(8,128)S(1)} %rep_sum.1.total) | copy-start | bytes 344068

commit v3 on v2

v3 whole, which is shorter than its diff:
```python
import functools

import jax
import jax.numpy as jnp
from jax import lax
from jax.experimental import pallas as pl
from jax.experimental.pallas import tpu as pltpu
from jax.sharding import PartitionSpec as P

RANK = 64
HALF = 32
LANES = 128
FLAT = RANK * RANK
CL_DEV = 4
SLOTS = 7
ROW_SLOTS = 9
COLUMNS = 3 * SLOTS + 2
GROUP = 8
MESH = pl.DeviceIdType.MESH
F32 = jnp.float32
BF16 = jnp.bfloat16
EXACT = lax.Precision.HIGHEST
WIDE = 256
BATCH = 25
MIB = 1024 * 1024


def lanes_left(rows):
    return lax.broadcasted_iota(jnp.int32, (rows, LANES), 1) < RANK


def swap(x):
    return pltpu.roll(x, RANK, 1)


def exact_dot(a, b):
    return jnp.dot(a, b, precision=EXACT, preferred_element_type=F32)


def exact_gram(a, b):
    return lax.dot_general(a, b, (((0,), (0,)), ((), ())), precision=EXACT, preferred_element_type=F32)


def flipped(index, bits):
    result = index
    for place in range(3):
        if bits >> place & 1:
            result = result + (1 - 2 * (index // (1 << place) % 2)) * (1 << place)
    return result


def tiles_of(flat, rows, lines):
    for tile in range(HALF):
        lines[tile * 8 : tile * 8 + rows, :] = flat[:, tile * LANES : (tile + 1) * LANES]


def packed(lines, which):
    return lines[pl.ds(which, HALF, stride=8), :]


def natural_pair(left, right, page):
    side = lanes_left(HALF)
    page[pl.ds(0, HALF, stride=2), :] = jnp.where(side, left, swap(right))
    page[pl.ds(1, HALF, stride=2), :] = jnp.where(side, swap(left), right)
    return page[...]


def pack(x):
    return jnp.concatenate([x[:HALF], x[HALF:]], axis=1)


def unpack(x):
    return jnp.concatenate([x[:, :RANK], x[:, RANK:]], axis=0)


def picked(x, index):
    return jnp.take_along_axis(x, index, axis=1, mode="promise_in_bounds")


def factorize(rows, upper):
    lane = lax.broadcasted_iota(jnp.int32, (8, LANES), 1)
    base = jnp.where(lane < RANK, 0, RANK)
    inner = lane - base
    all_rows = RANK * 8
    tall_base = jnp.where(lax.broadcasted_iota(jnp.int32, (all_rows, LANES), 1) < RANK, 0, RANK)
    tall_index = tall_base + lax.broadcasted_iota(jnp.int32, (all_rows, LANES), 0) // 8
    rest = jnp.concatenate(rows, axis=0)
    for panel in range(0, RANK, 8):
        block = [rest[r * 8 : (r + 1) * 8] for r in range(8)]
        rest = rest[RANK:] if panel + 8 < RANK else None
        entry = {}
        for r in range(8):
            for c in range(r, 8):
                entry[r, c] = picked(block[r], base + (panel + c))
        done = []
        for k in range(8):
            scale = lax.rsqrt(entry[k, k])
            done.append(block[k] * scale)
            for c in range(k + 1, 8):
                entry[k, c] = entry[k, c] * scale
            for r in range(k + 1, 8):
                block[r] = block[r] - entry[k, r] * done[k]
                for c in range(r, 8):
                    entry[r, c] = entry[r, c] - entry[k, r] * entry[k, c]
        if rest is not None:
            index = tall_index[RANK + panel * 8 :]
            for k in range(8):
                tall = jnp.concatenate([done[k]] * (RANK - panel - 8), axis=0)
                rest = rest - picked(tall, index) * tall
        for k in range(8):
            at = (panel + k) * 8
            upper[at : at + 8, :] = jnp.where(inner >= panel + k, done[k], 0.0)


def visit_order(admissible, leaf, padded_in, blocks, empty):
    padded_in[...] = jnp.full(padded_in.shape, -1, jnp.int32)
    padded_in[0:3, 0 : admissible.shape[1]] = admissible[...]
    level = padded_in[0:1, :]
    row = padded_in[1:2, :]
    column = padded_in[2:3, :]
    low = level <= 2
    base = jnp.where(level == 0, 0, jnp.where(level == 1, CL_DEV, CL_DEV + CL_DEV // 2))
    shift = jnp.where(level == 0, 2, jnp.where(level == 1, 1, 0))
    held = jnp.left_shift(1, shift) - 1
    slot = jnp.where(low, base + jnp.bitwise_and(row, held), level + (SLOTS - 3))
    slot = jnp.where(level < 0, -1, slot)
    side = jnp.minimum(jnp.maximum(jnp.right_shift(column, shift) - leaf + 1, 0), 2)
    place = jnp.where(
        low, side * SLOTS + base + jnp.bitwise_and(column, held), 3 * SLOTS + level - 3
    )
    member = lax.broadcasted_iota(jnp.int32, (16, WIDE), 0) == slot
    ahead = lax.broadcasted_iota(jnp.int32, (WIDE, WIDE), 0) <= lax.broadcasted_iota(
        jnp.int32, (WIDE, WIDE), 1
    )
    member_f = jnp.where(member, 1.0, 0.0).astype(F32)
    rank = jnp.dot(member_f.astype(BF16), jnp.where(ahead, 1.0, 0.0).astype(BF16), preferred_element_type=F32)
    count = jnp.sum(member_f, axis=1, keepdims=True)
    even = jnp.floor((count + 1.0) * 0.5) * 2.0
    even = jnp.broadcast_to(even, (16, WIDE)).astype(BF16)
    below = lax.broadcasted_iota(jnp.int32, (16, 16), 1) < lax.broadcasted_iota(jnp.int32, (16, 16), 0)
    begin = jnp.dot(jnp.where(below, 1.0, 0.0).astype(BF16), even, preferred_element_type=F32)
    at = jnp.sum(jnp.where(member, begin + rank - 1.0, 0.0), axis=0, keepdims=True)
    at = jnp.where(slot < 0, -1.0, at).astype(jnp.int32)
    chosen = lax.broadcasted_iota(jnp.int32, (WIDE, WIDE), 0) == at
    line = lax.broadcasted_iota(jnp.int32, (8, WIDE), 0)
    lane = lax.broadcasted_iota(jnp.int32, (8, WIDE), 1)
    values = jnp.where(line == 0, lane + 1, jnp.where(line == 1, place, jnp.where(line == 2, slot, 0)))
    listed = lax.dot_general(
        values.astype(F32).astype(BF16), jnp.where(chosen, 1.0, 0.0).astype(BF16),
        (((1,), (1,)), ((), ())), preferred_element_type=F32,
    )
    same = jnp.where(listed[2:3] == pltpu.roll(listed, 2, 1)[2:3], 1.0, 0.0)
    last = jnp.where(count > 0.0, (begin + even.astype(F32)) * 0.5 - 1.0, float(empty))
    diagonal = lax.broadcasted_iota(jnp.int32, (16, WIDE), 0) == lax.broadcasted_iota(
        jnp.int32, (16, WIDE), 1
    )
    last = jnp.sum(jnp.where(diagonal, last, 0.0), axis=0, keepdims=True)
    listed = jnp.where(line == 3, same, jnp.where(line == 4, last, listed))
    listed = jnp.where(line == 5, at, listed.astype(jnp.int32))
    limits = (blocks, COLUMNS - 1, ROW_SLOTS - 1, 1, empty, 2 * empty - 1)
    limit = jnp.zeros(line.shape, jnp.int32)
    for k, most in enumerate(limits):
        limit = jnp.where(line == k, most, limit)
    return jnp.minimum(jnp.maximum(listed, 0), limit)


def main_kernel(
    leaves, reps, blocks, chunk, pairs,
    order_in, bottom_in, zero_in, one_in, two_in, three_in, admissible_in, coupling_in,
    projected_to, weights_zero, weights_one, weights_two,
    child, bottom, zero, one, two, three, admissible, coupling, projected, zero_v, one_v, two_v,
    lines, lines_three, page, kids, factors, near, tops, grams, upper,
    padded_in, visits_v, order, row_table, column_left, column_right,
    own, turned, results, snapshots, parts, total,
    fetched, stored, order_sem, send, receive, share_send, share_receive,
):
    me = lax.axis_index("leaf")
    rep = lax.axis_index("rep")
    left = lax.rem(me + leaves - 1, leaves)
    right = lax.rem(me + 1, leaves)
    others = [flipped(me, bits) for bits in range(1, GROUP)]
    start = pl.multiple_of(me // 2 // chunk * chunk, chunk)
    fetches = [
        pltpu.make_async_copy(source, target, fetched.at[k])
        for k, (source, target) in enumerate((
            (bottom_in, bottom), (zero_in, zero), (order_in, child), (one_in, one), (two_in, two),
            (three_in.at[pl.ds(start, chunk)], three), (admissible_in, admissible),
            (coupling_in, coupling),
        ))
    ]
    for fetch in fetches:
        fetch.start()
    barrier = pltpu.get_barrier_semaphore()
    for other in [left, right] + others:
        pl.semaphore_signal(barrier, inc=1, device_id=(other, rep), device_id_type=MESH)
    for step in range(1, reps):
        other = lax.rem(rep + step, reps)
        pl.semaphore_signal(barrier, inc=1, device_id=(me, other), device_id_type=MESH)
    for fetch in fetches[:5]:
        fetch.wait()

    tiles_of(bottom, CL_DEV, lines)
    bottoms = [packed(lines, c) for c in range(CL_DEV)]
    leaf_pairs = [natural_pair(bottoms[c], bottoms[c + 1], page) for c in (0, 2)]
    for k in range(2):
        factors[1, k * RANK : (k + 1) * RANK, :] = leaf_pairs[k].astype(BF16)
    tiles_of(zero, CL_DEV, lines)
    zeros = [packed(lines, c) for c in range(CL_DEV)]
    zero_pairs = [natural_pair(zeros[c], zeros[c + 1], page) for c in (0, 2)]
    tiles_of(one, CL_DEV // 2, lines)
    ones = natural_pair(packed(lines, 0), packed(lines, 1), page)
    tiles_of(two, 1, lines)
    own_two = packed(lines, 0)
    twos = natural_pair(own_two, own_two, page)[:, :RANK]

    for c in range(CL_DEV):
        half = slice(c % 2 * RANK, c % 2 * RANK + RANK)
        image = exact_dot(leaf_pairs[c // 2][:, half], zero_pairs[c // 2][:, half])
        kids[c] = exact_gram(image, image)
    level_one = [kids[child[0, 2 * i]] + kids[child[0, 2 * i + 1]] for i in range(2)]
    near[1, :RANK, :] = jnp.concatenate(level_one, axis=1)
    level_two = 0.0
    for i in range(2):
        transfer = ones[:, i * RANK : (i + 1) * RANK]
        level_two = level_two + exact_gram(transfer, exact_dot(level_one[i], transfer))
    near[1, RANK:, :] = pack(level_two)
    tops[0] = pack(exact_gram(twos, exact_dot(level_two, twos)))

    pl.semaphore_wait(barrier, GROUP + reps)
    copies = []

    def push(source, target, device):
        place = len(copies)
        copy = pltpu.make_async_remote_copy(
            src_ref=source, dst_ref=target, send_sem=send.at[place], recv_sem=receive.at[place],
            device_id=(device, rep), device_id_type=MESH,
        )
        copy.start()
        copies.append(copy)

    for bits in range(1, GROUP):
        push(tops.at[0], tops.at[bits], others[bits - 1])
    push(near.at[1], near.at[2], left)
    push(near.at[1], near.at[0], right)
    push(factors.at[1], factors.at[2], left)
    push(factors.at[1], factors.at[0], right)

    fetches[6].wait()
    visits_v[...] = visit_order(admissible, me, padded_in, blocks, pairs)
    to_scalar = pltpu.make_async_copy(visits_v, order, order_sem)
    to_scalar.start()
    fetches[7].wait()
    own[0] = jnp.zeros((HALF, LANES), BF16)
    turned[0] = jnp.zeros((HALF, LANES), BF16)

    def lay(group, carry):
        first = pl.multiple_of(group * 16, 16)
        x = coupling[pl.ds(first, 16), :].astype(F32)
        for h in range(2):
            for tile in range(HALF):
                at = (h * HALF + tile) * 8
                lines[at : at + 8, :] = x[8 * h : 8 * h + 8, tile * LANES : (tile + 1) * LANES]
        for s in range(16):
            block = lines[pl.ds(s // 8 * 256 + s % 8, HALF, stride=8), :]
            own[first + s + 1] = block.astype(BF16)
            turned[first + s + 1] = swap(block).astype(BF16)
        return carry

    lax.fori_loop(0, blocks // 16, lay, 0)

    fetches[5].wait()
    tiles_of(three, chunk, lines_three)
    place = lax.rem(me // 2, chunk)
    threes = []
    for u in range(GROUP // 2):
        matrix = packed(lines_three, flipped(place, u))
        threes.append(natural_pair(matrix, matrix, page)[:, :RANK])
    for copy in copies[: GROUP - 1]:
        copy.wait_recv()
    level_three, lifted = [], []
    for u in range(GROUP // 2):
        gram = unpack(tops[2 * u] + tops[2 * u + 1])
        level_three.append(gram)
        lifted.append(exact_gram(threes[u], exact_dot(gram, threes[u])))
    level_four = [lifted[0] + lifted[1], lifted[2] + lifted[3]]
    for copy in copies[GROUP - 1 :]:
        copy.wait_recv()
    for side in range(3):
        grams[side * RANK : (side + 1) * RANK, :] = near[side, :RANK, :]
    side_two = [unpack(near[side, RANK:, :]) for side in range(3)]
    rest = side_two + [level_three[0], level_three[1], level_four[0], level_four[1], level_four[1]]
    for k in range(4):
        at = (3 + k) * RANK
        grams[at : at + RANK, :] = jnp.concatenate([rest[2 * k], rest[2 * k + 1]], axis=1)
    grams[7 * RANK :, :] = near[1, :RANK, :]

    side = lanes_left(HALF)
    side_full = lanes_left(RANK)
    lane = lax.broadcasted_iota(jnp.int32, (RANK, LANES), 1)
    inner = jnp.where(lane < RANK, lane, lane - RANK)
    spread = jnp.where(inner < HALF, 2 * inner, 2 * inner - (RANK - 1)) + (lane - inner)

    factorize([grams[pl.ds(i, 8, stride=RANK), :] for i in range(RANK)], upper)

    def put_column(where, left, right):
        column_left[where] = left.astype(BF16)
        column_right[where] = right.astype(BF16)

    def put_columns(first, second, names):
        flipped_all = jnp.transpose(jnp.concatenate([first, second], axis=0))
        for half in range(2):
            part = flipped_all[half * RANK : (half + 1) * RANK]
            other = swap(part)
            if names[half] is not None:
                put_column(names[half], jnp.where(side_full, part, 0.0), jnp.where(side_full, 0.0, other))
            if names[2 + half] is not None:
                put_column(names[2 + half], jnp.where(side_full, other, 0.0), jnp.where(side_full, 0.0, part))

    def put_rows(even, odd, names):
        x = picked(jnp.concatenate([even, odd], axis=0), spread)
        if names[0] is not None:
            row_table[names[0]] = x.astype(BF16)
        if names[1] is not None:
            row_table[names[1]] = swap(x).astype(BF16)

    for near_by in range(3):
        first = factors[near_by, :RANK, :].astype(F32)
        second = factors[near_by, RANK:, :].astype(F32)
        put_columns(first, second, [near_by * SLOTS + c for c in (0, 1, 2, 3)])
        if near_by == 1:
            for k, x in enumerate((first, second)):
                lines[k * RANK : (k + 1) * RANK, :] = x
                put_rows(
                    lines[pl.ds(k * RANK, HALF, stride=2), :],
                    lines[pl.ds(k * RANK + 1, HALF, stride=2), :],
                    (2 * k, 2 * k + 1),
                )
    column_names = [
        (4, 5), (SLOTS + 4, SLOTS + 5), (2 * SLOTS + 4, 2 * SLOTS + 5), (6, SLOTS + 6),
        (2 * SLOTS + 6, None), (3 * SLOTS, None), (3 * SLOTS + 1, None), (None, None),
    ]
    for k in range(0, 8, 2):
        put_columns(
            upper[pl.ds(k, RANK, stride=8), :], upper[pl.ds(k + 1, RANK, stride=8), :],
            column_names[k] + column_names[k + 1],
        )
    for k, names in ((1, (4, 5)), (3, (None, 6)), (4, (None, 7)), (5, (None, 8))):
        put_rows(upper[pl.ds(k, HALF, stride=16), :], upper[pl.ds(8 + k, HALF, stride=16), :], names)

    snapshots[pairs] = jnp.zeros((RANK, LANES), F32)
    to_scalar.wait()

    def visits(step, carry):
        places = [step * BATCH + k for k in range(BATCH)]
        halves = []
        for pair in places:
            a, b = order[0, 2 * pair], order[0, 2 * pair + 1]
            both = jnp.concatenate(
                [jnp.where(side, own[a], turned[b]), jnp.where(side, turned[a], own[b])], axis=0
            )
            slot = order[2, 2 * pair]
            halves.append(
                jnp.dot(row_table[slot][:, :RANK], both, preferred_element_type=F32).astype(BF16)
            )
        products = []
        for pair, half in zip(places, halves):
            columns = jnp.concatenate(
                [column_left[order[1, 2 * pair]], column_right[order[1, 2 * pair + 1]]], axis=0
            )
            products.append(jnp.dot(half, columns, preferred_element_type=F32))
        terms = []
        for product in products:
            rounded = product.astype(BF16)
            terms.append(lax.dot_general(
                rounded, rounded, (((1,), (1,)), ((), ())), preferred_element_type=F32
            ))
        for pair, result in zip(places, products):
            top, bottom_half = result[:HALF], result[HALF:]
            results[2 * pair] = jnp.where(side, top, swap(bottom_half))
            results[2 * pair + 1] = jnp.where(side, swap(top), bottom_half)
        for pair, term in zip(places, terms):
            carry = carry * order[3, 2 * pair].astype(F32) + term
            snapshots[pair, :, :RANK] = carry
        return carry

    lax.fori_loop(0, pairs // BATCH, visits, jnp.zeros((RANK, RANK), F32))

    gather = jnp.where(inner % 2 == 0, inner // 2, HALF + inner // 2)
    for s in range(SLOTS):
        x = picked(snapshots[order[4, s]], gather)
        part = jnp.where(side, x[:HALF], x[HALF:]) * (1.0 / RANK)
        parts[rep, s * HALF : (s + 1) * HALF, :] = part.astype(BF16)
    shares = []
    for step in range(1, reps):
        copy = pltpu.make_async_remote_copy(
            src_ref=parts.at[rep], dst_ref=parts.at[rep],
            send_sem=share_send.at[step - 1], recv_sem=share_receive.at[step - 1],
            device_id=(me, lax.rem(rep + step, reps)), device_id_type=MESH,
        )
        copy.start()
        shares.append(copy)

    def store_of(group):
        span = pl.ds(pl.multiple_of(group * 16, 16), 16)
        return pltpu.make_async_copy(projected.at[span], projected_to.at[span], stored.at[group])

    def write(group, carry):
        first = pl.multiple_of(group * 16, 16)
        for s in range(16):
            lines[s * HALF : (s + 1) * HALF, :] = results[order[5, first + s]]
        for tile in range(HALF):
            x = jnp.concatenate(
                [
                    lines[pl.ds(tile, 8, stride=HALF), :],
                    lines[pl.ds(tile + 8 * HALF, 8, stride=HALF), :],
                ],
                axis=0,
            )
            projected[pl.ds(first, 16), tile * LANES : (tile + 1) * LANES] = x.astype(BF16)
        store_of(group).start()
        return carry

    groups = blocks // 16
    lax.fori_loop(0, groups, write, 0)
    for copy in shares:
        copy.wait_recv()
    added = parts[0].astype(F32)
    for k in range(1, reps):
        added = added + parts[k].astype(F32)
    total[...] = added
    for tile in range(HALF):
        span = slice(tile * LANES, (tile + 1) * LANES)
        zero_v[:, span] = total[pl.ds(tile, CL_DEV, stride=HALF), :]
        one_v[:, span] = total[pl.ds(tile + CL_DEV * HALF, CL_DEV // 2, stride=HALF), :]
        at = tile + (SLOTS - 1) * HALF
        two_v[:, span] = total[at : at + 1, :]
    stores = [
        pltpu.make_async_copy(source, target, stored.at[groups + k])
        for k, (source, target) in enumerate(
            ((zero_v, weights_zero), (one_v, weights_one), (two_v, weights_two))
        )
    ]
    for store in stores:
        store.start()
    for copy in copies + shares:
        copy.wait_send()
    for store in stores + [store_of(group) for group in range(groups)]:
        store.wait()


def main_call(leaves, reps, order, bottom, zero, one, two, three, admissible, coupling):
    chunk = min(8, three.shape[0])
    blocks = coupling.shape[0]
    pairs = (blocks + ROW_SLOTS) // 2
    pairs = -(-pairs // BATCH) * BATCH
    hbm = pl.BlockSpec(memory_space=pltpu.HBM)
    small = [jax.ShapeDtypeStruct((count, FLAT), F32) for count in (CL_DEV, CL_DEV // 2, 1)]
    count = GROUP + 3
    whole = [bottom, zero, one, two]
    return pl.pallas_call(
        functools.partial(main_kernel, leaves, reps, blocks, chunk, pairs),
        out_shape=[jax.ShapeDtypeStruct((blocks, FLAT), BF16)] + small,
        in_specs=[hbm] * 8,
        out_specs=[hbm] * 4,
        scratch_shapes=[
            pltpu.SMEM(order.shape, jnp.int32),
            *[pltpu.VMEM(x.shape, x.dtype) for x in whole],
            pltpu.VMEM((chunk, FLAT), F32),
            pltpu.VMEM(admissible.shape, jnp.int32),
            pltpu.VMEM(coupling.shape, BF16),
            pltpu.VMEM(coupling.shape, BF16),
            *[pltpu.VMEM(x.shape, F32) for x in small],
            pltpu.VMEM((512, LANES), F32),
            pltpu.VMEM((HALF * 8, LANES), F32),
            pltpu.VMEM((RANK, LANES), F32),
            pltpu.VMEM((CL_DEV, RANK, RANK), F32),
            pltpu.VMEM((3, LANES, LANES), BF16),
            pltpu.VMEM((3, RANK + HALF, LANES), F32),
            pltpu.VMEM((GROUP, HALF, LANES), F32),
            pltpu.VMEM((8 * RANK, LANES), F32),
            pltpu.VMEM((8 * RANK, LANES), F32),
            pltpu.VMEM((8, WIDE), jnp.int32),
            pltpu.VMEM((8, WIDE), jnp.int32),
            pltpu.SMEM((8, WIDE), jnp.int32),
            pltpu.VMEM((ROW_SLOTS, RANK, LANES), BF16),
            pltpu.VMEM((COLUMNS, RANK, LANES), BF16),
            pltpu.VMEM((COLUMNS, RANK, LANES), BF16),
            pltpu.VMEM((blocks + 1, HALF, LANES), BF16),
            pltpu.VMEM((blocks + 1, HALF, LANES), BF16),
            pltpu.VMEM((2 * pairs, HALF, LANES), F32),
            pltpu.VMEM((pairs + 1, RANK, LANES), F32),
            pltpu.VMEM((reps, SLOTS * HALF, LANES), BF16),
            pltpu.VMEM((SLOTS * HALF, LANES), F32),
            pltpu.SemaphoreType.DMA((8,)),
            pltpu.SemaphoreType.DMA((blocks // 16 + 3,)),
            pltpu.SemaphoreType.DMA,
            pltpu.SemaphoreType.DMA((count,)),
            pltpu.SemaphoreType.DMA((count,)),
            pltpu.SemaphoreType.DMA((reps - 1,)),
            pltpu.SemaphoreType.DMA((reps - 1,)),
        ],
        compiler_params=pltpu.CompilerParams(
            collective_id=0, has_side_effects=True, vmem_limit_bytes=60 * MIB
        ),
        name="upsweep_and_blocks",
    )(order, bottom, zero, one, two, three, admissible, coupling)


def deliver_kernel(parts, *refs):
    count = len(refs) // 3
    sources, targets, held = refs[:count], refs[count : 2 * count], refs[2 * count : 3 * count]
    came, went = refs[3 * count :]
    rows = sources[0].shape[0] // parts
    spans = [(0, pl.ds(k * rows, rows)) for k in range(parts)]
    spans += [(k, pl.ds(0, sources[k].shape[0])) for k in range(1, count)]
    reads = [
        pltpu.make_async_copy(sources[k].at[span], held[k].at[span], came.at[n])
        for n, (k, span) in enumerate(spans)
    ]
    writes = [
        pltpu.make_async_copy(held[k].at[span], targets[k].at[span], went.at[n])
        for n, (k, span) in enumerate(spans)
    ]
    for read in reads:
        read.start()
    for read, write in zip(reads, writes):
        read.wait()
        write.start()
    for write in writes:
        write.wait()


def deliver_call(*arrays):
    hbm = pl.BlockSpec(memory_space=pltpu.HBM)
    parts = 4
    moves = len(arrays) - 1 + parts
    return pl.pallas_call(
        functools.partial(deliver_kernel, parts),
        out_shape=[jax.ShapeDtypeStruct(x.shape, x.dtype) for x in arrays],
        in_specs=[hbm] * len(arrays),
        out_specs=[hbm] * len(arrays),
        scratch_shapes=[pltpu.VMEM(x.shape, x.dtype) for x in arrays]
        + [pltpu.SemaphoreType.DMA((moves,))] * 2,
        compiler_params=pltpu.CompilerParams(vmem_limit_bytes=60 * MIB),
        name="deliver",
    )(*arrays)


def local(leaves, reps, bottom, zero, one, two, three, order, coupling, admissible):
    return tuple(deliver_call(
        *main_call(leaves, reps, order, bottom, zero, one, two, three, admissible, coupling)
    ))


def solution(mesh):
    return jax.shard_map(
        functools.partial(local, mesh.shape["leaf"], mesh.shape["rep"]),
        mesh=mesh,
        in_specs=(
            P("leaf", None),
            P("leaf", None),
            P("leaf", None),
            P("leaf", None),
            P(),
            P("leaf", None),
            P(("leaf", "rep"), None),
            P(None, ("leaf", "rep")),
        ),
        out_specs=(P(("leaf", "rep"), None), P("leaf", None), P("leaf", None), P("leaf", None)),
        check_vma=False,
    )
```

time: 43.9 us -> 35.5 us (0.81)
  the two profiles are of different devices: /device:TPU:4 before, /device:TPU:2 now
where the time goes in v3:
time: 35.5 us; the launch traced here: 35.3 us
  Pallas kernels  34.7 us (98%)
  between operations  0.64 us (2%)
    pallas_call x1, Pallas kernels, main_call(): pl.pallas_call(functools.partial(main_kernel, leaves, reps, blocks, chunk...  32.4 us
    pallas_call x1, Pallas kernels, deliver_call(): pl.pallas_call(functools.partial(deliver_kernel, parts), out_shape=[jax.S...  2.27 us

profile of v3, /device:TPU:2, one launch (start us, length us, event | category | flops | bytes accessed | tf_op | source)
XLA Modules:
  0.0 35.3 jit_solution(16247220044771662016)
XLA Ops:
  0.6 32.4 %upsweep_and_blocks.1 = (bf16[192,4096]{1,0:T(8,128)(2,1)}, f32[4,4096]{1,0:T(4,128)}, f32[2,4096]{1,0:T(2,128)}, f32[1,4096]{1,0:T(1,128)}) custom-call(s32[1,4]{1,0:T(1,128)} %order_in.1, f32[4,4096]{1,0:T(4,128)} %bottom_in.1, f32[4,4096]{1,0:T(4,128)} %zero_in.1, f32[2,4096]{1,0:T(2,128)} %one_in.1, f32[1,4096]{1,0:T(1,128)} %two_in.1, ...), custom_call_target="tpu_custom_call" | custom-call | tf_op jit(solution)/shard_map/upsweep_and_blocks/pallas_call | solution.py:460
  33.1 2.3 %deliver.1 = (bf16[192,4096]{1,0:T(8,128)(2,1)}, f32[4,4096]{1,0:T(4,128)}, f32[2,4096]{1,0:T(2,128)}, f32[1,4096]{1,0:T(1,128)}) custom-call(bf16[192,4096]{1,0:T(8,128)(2,1)} %get-tuple-element.8.refs_0_, f32[4,4096]{1,0:T(4,128)} %get-tuple-element.9.refs_1_, f32[2,4096]{1,0:T(2,128)} %get-tuple-element.10.refs_2_, f32[1,4096]{1,0:T(1,128)} %get-tuple-element.11.refs_3_), custom_call_target="tpu_custom_call" | custom-call | tf_op jit(solution)/shard_map/deliver/pallas_call | solution.py:537

commit v4 on v3

--- a/solution.py
+++ b/solution.py
@@ -21,7 +21,9 @@
 BF16 = jnp.bfloat16
 EXACT = lax.Precision.HIGHEST
 WIDE = 256
-BATCH = 25
+BATCH = 100
+PITCH = 72
+APART = 40
 MIB = 1024 * 1024
 
 
@@ -77,21 +79,20 @@
     return jnp.take_along_axis(x, index, axis=1, mode="promise_in_bounds")
 
 
-def factorize(rows, upper):
+def added(terms):
+    while len(terms) > 1:
+        terms = [sum(terms[k + 1 : k + 2], terms[k]) for k in range(0, len(terms), 2)]
+    return terms[0]
+
+
+def factorize_rows(rows, first, last, upper):
     lane = lax.broadcasted_iota(jnp.int32, (8, LANES), 1)
     base = jnp.where(lane < RANK, 0, RANK)
     inner = lane - base
-    all_rows = RANK * 8
-    tall_base = jnp.where(lax.broadcasted_iota(jnp.int32, (all_rows, LANES), 1) < RANK, 0, RANK)
-    tall_index = tall_base + lax.broadcasted_iota(jnp.int32, (all_rows, LANES), 0) // 8
-    rest = jnp.concatenate(rows, axis=0)
-    for panel in range(0, RANK, 8):
-        block = [rest[r * 8 : (r + 1) * 8] for r in range(8)]
-        rest = rest[RANK:] if panel + 8 < RANK else None
-        entry = {}
-        for r in range(8):
-            for c in range(r, 8):
-                entry[r, c] = picked(block[r], base + (panel + c))
+    pivots = [(r, c) for r in range(8) for c in range(r, 8)]
+    entry = {(r, c): picked(rows[first + r], base + (first + c)) for r, c in pivots}
+    for panel in range(first, last, 8):
+        block = rows[panel : panel + 8]
         done = []
         for k in range(8):
             scale = lax.rsqrt(entry[k, k])
@@ -102,14 +103,39 @@
                 block[r] = block[r] - entry[k, r] * done[k]
                 for c in range(r, 8):
                     entry[r, c] = entry[r, c] - entry[k, r] * entry[k, c]
-        if rest is not None:
-            index = tall_index[RANK + panel * 8 :]
-            for k in range(8):
-                tall = jnp.concatenate([done[k]] * (RANK - panel - 8), axis=0)
-                rest = rest - picked(tall, index) * tall
+        after = panel + 8
+        if after < last:
+            old = {(r, c): picked(rows[after + r], base + (after + c)) for r, c in pivots}
+            near = [[picked(done[k], base + (after + j)) for j in range(8)] for k in range(8)]
+            entry = {
+                (r, c): old[r, c] - added([near[k][r] * near[k][c] for k in range(8)])
+                for r, c in pivots
+            }
+            for r in range(8):
+                rows[after + r] = rows[after + r] - added([near[k][r] * done[k] for k in range(8)])
+            for i in range(after + 8, last):
+                rows[i] = rows[i] - added([picked(done[k], base + i) * done[k] for k in range(8)])
         for k in range(8):
             at = (panel + k) * 8
             upper[at : at + 8, :] = jnp.where(inner >= panel + k, done[k], 0.0)
+
+
+def factorize(grams, upper, used):
+    rows = [grams[pl.ds(i, 8, stride=PITCH), :] for i in range(RANK)]
+    factorize_rows(rows, 0, HALF, upper)
+    side = lanes_left(HALF)
+    for pair in range(used):
+        top = upper[pl.ds(pair, HALF, stride=8), :]
+        turned_top = jnp.transpose(top)
+        both = jnp.concatenate([turned_top[HALF:RANK], turned_top[RANK + HALF :]], axis=0)
+        taken = exact_dot(both, top)
+        at = pair * PITCH + HALF
+        grams[at : at + HALF, :] = grams[at : at + HALF, :] - jnp.where(
+            side, taken[:HALF], taken[HALF:]
+        )
+    for i in range(HALF, RANK):
+        rows[i] = grams[pl.ds(i, 8, stride=PITCH), :]
+    factorize_rows(rows, HALF, RANK, upper)
 
 
 def visit_order(admissible, leaf, padded_in, blocks, empty):
@@ -266,7 +292,7 @@
             turned[first + s + 1] = swap(block).astype(BF16)
         return carry
 
-    lax.fori_loop(0, blocks // 16, lay, 0)
+    lax.fori_loop(0, blocks // 16, lay, 0, unroll=2)
 
     fetches[5].wait()
     tiles_of(three, chunk, lines_three)
@@ -286,13 +312,13 @@
     for copy in copies[GROUP - 1 :]:
         copy.wait_recv()
     for side in range(3):
-        grams[side * RANK : (side + 1) * RANK, :] = near[side, :RANK, :]
+        grams[side * PITCH : side * PITCH + RANK, :] = near[side, :RANK, :]
     side_two = [unpack(near[side, RANK:, :]) for side in range(3)]
     rest = side_two + [level_three[0], level_three[1], level_four[0], level_four[1], level_four[1]]
     for k in range(4):
-        at = (3 + k) * RANK
+        at = (3 + k) * PITCH
         grams[at : at + RANK, :] = jnp.concatenate([rest[2 * k], rest[2 * k + 1]], axis=1)
-    grams[7 * RANK :, :] = near[1, :RANK, :]
+    grams[7 * PITCH : 7 * PITCH + RANK, :] = near[1, :RANK, :]
 
     side = lanes_left(HALF)
     side_full = lanes_left(RANK)
@@ -300,7 +326,7 @@
     inner = jnp.where(lane < RANK, lane, lane - RANK)
     spread = jnp.where(inner < HALF, 2 * inner, 2 * inner - (RANK - 1)) + (lane - inner)
 
-    factorize([grams[pl.ds(i, 8, stride=RANK), :] for i in range(RANK)], upper)
+    factorize(grams, upper, 7)
 
     def put_column(where, left, right):
         column_left[where] = left.astype(BF16)
@@ -407,12 +433,12 @@
     def write(group, carry):
         first = pl.multiple_of(group * 16, 16)
         for s in range(16):
-            lines[s * HALF : (s + 1) * HALF, :] = results[order[5, first + s]]
+            lines[s * APART : s * APART + HALF, :] = results[order[5, first + s]]
         for tile in range(HALF):
             x = jnp.concatenate(
                 [
-                    lines[pl.ds(tile, 8, stride=HALF), :],
-                    lines[pl.ds(tile + 8 * HALF, 8, stride=HALF), :],
+                    lines[pl.ds(tile, 8, stride=APART), :],
+                    lines[pl.ds(tile + 8 * APART, 8, stride=APART), :],
                 ],
                 axis=0,
             )
@@ -424,15 +450,16 @@
     lax.fori_loop(0, groups, write, 0)
     for copy in shares:
         copy.wait_recv()
-    added = parts[0].astype(F32)
+    added_up = parts[0].astype(F32)
     for k in range(1, reps):
-        added = added + parts[k].astype(F32)
-    total[...] = added
+        added_up = added_up + parts[k].astype(F32)
+    for s in range(SLOTS):
+        total[s * APART : s * APART + HALF, :] = added_up[s * HALF : (s + 1) * HALF]
     for tile in range(HALF):
         span = slice(tile * LANES, (tile + 1) * LANES)
-        zero_v[:, span] = total[pl.ds(tile, CL_DEV, stride=HALF), :]
-        one_v[:, span] = total[pl.ds(tile + CL_DEV * HALF, CL_DEV // 2, stride=HALF), :]
-        at = tile + (SLOTS - 1) * HALF
+        zero_v[:, span] = total[pl.ds(tile, CL_DEV, stride=APART), :]
+        one_v[:, span] = total[pl.ds(tile + CL_DEV * APART, CL_DEV // 2, stride=APART), :]
+        at = tile + (SLOTS - 1) * APART
         two_v[:, span] = total[at : at + 1, :]
     stores = [
         pltpu.make_async_copy(source, target, stored.at[groups + k])
@@ -470,14 +497,14 @@
             pltpu.VMEM(coupling.shape, BF16),
             pltpu.VMEM(coupling.shape, BF16),
             *[pltpu.VMEM(x.shape, F32) for x in small],
-            pltpu.VMEM((512, LANES), F32),
+            pltpu.VMEM((640, LANES), F32),
             pltpu.VMEM((HALF * 8, LANES), F32),
             pltpu.VMEM((RANK, LANES), F32),
             pltpu.VMEM((CL_DEV, RANK, RANK), F32),
             pltpu.VMEM((3, LANES, LANES), BF16),
             pltpu.VMEM((3, RANK + HALF, LANES), F32),
             pltpu.VMEM((GROUP, HALF, LANES), F32),
-            pltpu.VMEM((8 * RANK, LANES), F32),
+            pltpu.VMEM((8 * PITCH, LANES), F32),
             pltpu.VMEM((8 * RANK, LANES), F32),
             pltpu.VMEM((8, WIDE), jnp.int32),
             pltpu.VMEM((8, WIDE), jnp.int32),
@@ -490,7 +517,7 @@
             pltpu.VMEM((2 * pairs, HALF, LANES), F32),
             pltpu.VMEM((pairs + 1, RANK, LANES), F32),
             pltpu.VMEM((reps, SLOTS * HALF, LANES), BF16),
-            pltpu.VMEM((SLOTS * HALF, LANES), F32),
+            pltpu.VMEM((SLOTS * APART, LANES), F32),
             pltpu.SemaphoreType.DMA((8,)),
             pltpu.SemaphoreType.DMA((blocks // 16 + 3,)),
             pltpu.SemaphoreType.DMA,

time: 35.5 us -> 31.6 us (0.89)
  Pallas kernels: 34.7 us -> 30.8 us
    pallas_call x1, Pallas kernels: 32.4 us -> 28.6 us  [main_call(): pl.pallas_call(functools.partial(main_kernel, leaves, reps, blocks, chunk...]
where the time goes in v4:
time: 31.6 us; the launch traced here: 31.5 us
  Pallas kernels  30.8 us (97%)
  between operations  0.64 us (2%)
    pallas_call x1, Pallas kernels, main_call(): pl.pallas_call(functools.partial(main_kernel, leaves, reps, blocks, chunk...  28.6 us
    pallas_call x1, Pallas kernels, deliver_call(): pl.pallas_call(functools.partial(deliver_kernel, parts), out_shape=[jax.S...  2.27 us

profile of v4, /device:TPU:2, one launch (start us, length us, event | category | flops | bytes accessed | tf_op | source)
XLA Modules:
  0.0 31.5 jit_solution(2884615262934648824)
XLA Ops:
  0.6 28.6 %upsweep_and_blocks.1 = (bf16[192,4096]{1,0:T(8,128)(2,1)}, f32[4,4096]{1,0:T(4,128)}, f32[2,4096]{1,0:T(2,128)}, f32[1,4096]{1,0:T(1,128)}) custom-call(s32[1,4]{1,0:T(1,128)} %order_in.1, f32[4,4096]{1,0:T(4,128)} %bottom_in.1, f32[4,4096]{1,0:T(4,128)} %zero_in.1, f32[2,4096]{1,0:T(2,128)} %one_in.1, f32[1,4096]{1,0:T(1,128)} %two_in.1, ...), custom_call_target="tpu_custom_call" | custom-call | tf_op jit(solution)/shard_map/upsweep_and_blocks/pallas_call | solution.py:487
  29.2 2.3 %deliver.1 = (bf16[192,4096]{1,0:T(8,128)(2,1)}, f32[4,4096]{1,0:T(4,128)}, f32[2,4096]{1,0:T(2,128)}, f32[1,4096]{1,0:T(1,128)}) custom-call(bf16[192,4096]{1,0:T(8,128)(2,1)} %get-tuple-element.8.refs_0_, f32[4,4096]{1,0:T(4,128)} %get-tuple-element.9.refs_1_, f32[2,4096]{1,0:T(2,128)} %get-tuple-element.10.refs_2_, f32[1,4096]{1,0:T(1,128)} %get-tuple-element.11.refs_3_), custom_call_target="tpu_custom_call" | custom-call | tf_op jit(solution)/shard_map/deliver/pallas_call | solution.py:564

commit v5 on v4

--- a/solution.py
+++ b/solution.py
@@ -21,7 +21,6 @@
 BF16 = jnp.bfloat16
 EXACT = lax.Precision.HIGHEST
 WIDE = 256
-BATCH = 100
 PITCH = 72
 APART = 40
 MIB = 1024 * 1024
@@ -161,7 +160,7 @@
     member_f = jnp.where(member, 1.0, 0.0).astype(F32)
     rank = jnp.dot(member_f.astype(BF16), jnp.where(ahead, 1.0, 0.0).astype(BF16), preferred_element_type=F32)
     count = jnp.sum(member_f, axis=1, keepdims=True)
-    even = jnp.floor((count + 1.0) * 0.5) * 2.0
+    even = jnp.floor((count + 3.0) * 0.25) * 4.0
     even = jnp.broadcast_to(even, (16, WIDE)).astype(BF16)
     below = lax.broadcasted_iota(jnp.int32, (16, 16), 1) < lax.broadcasted_iota(jnp.int32, (16, 16), 0)
     begin = jnp.dot(jnp.where(below, 1.0, 0.0).astype(BF16), even, preferred_element_type=F32)
@@ -175,15 +174,15 @@
         values.astype(F32).astype(BF16), jnp.where(chosen, 1.0, 0.0).astype(BF16),
         (((1,), (1,)), ((), ())), preferred_element_type=F32,
     )
-    same = jnp.where(listed[2:3] == pltpu.roll(listed, 2, 1)[2:3], 1.0, 0.0)
-    last = jnp.where(count > 0.0, (begin + even.astype(F32)) * 0.5 - 1.0, float(empty))
+    same = jnp.where(listed[2:3] == pltpu.roll(listed, 4, 1)[2:3], 1.0, 0.0)
+    last = jnp.where(count > 0.0, (begin + even.astype(F32)) * 0.25 - 1.0, float(empty))
     diagonal = lax.broadcasted_iota(jnp.int32, (16, WIDE), 0) == lax.broadcasted_iota(
         jnp.int32, (16, WIDE), 1
     )
     last = jnp.sum(jnp.where(diagonal, last, 0.0), axis=0, keepdims=True)
     listed = jnp.where(line == 3, same, jnp.where(line == 4, last, listed))
     listed = jnp.where(line == 5, at, listed.astype(jnp.int32))
-    limits = (blocks, COLUMNS - 1, ROW_SLOTS - 1, 1, empty, 2 * empty - 1)
+    limits = (blocks, COLUMNS - 1, ROW_SLOTS - 1, 1, empty, 4 * empty - 1)
     limit = jnp.zeros(line.shape, jnp.int32)
     for k, most in enumerate(limits):
         limit = jnp.where(line == k, most, limit)
@@ -191,13 +190,13 @@
 
 
 def main_kernel(
-    leaves, reps, blocks, chunk, pairs,
+    leaves, reps, blocks, chunk, fours,
     order_in, bottom_in, zero_in, one_in, two_in, three_in, admissible_in, coupling_in,
-    projected_to, weights_zero, weights_one, weights_two,
-    child, bottom, zero, one, two, three, admissible, coupling, projected, zero_v, one_v, two_v,
+    projected_to, parts_to,
+    child, bottom, zero, one, two, three, admissible, coupling, projected,
     lines, lines_three, page, kids, factors, near, tops, grams, upper,
     padded_in, visits_v, order, row_table, column_left, column_right,
-    own, turned, results, snapshots, parts, total,
+    own, turned, results, snapshots, share,
     fetched, stored, order_sem, send, receive, share_send, share_receive,
 ):
     me = lax.axis_index("leaf")
@@ -217,12 +216,21 @@
     for fetch in fetches:
         fetch.start()
     barrier = pltpu.get_barrier_semaphore()
-    for other in [left, right] + others:
+    for other in others:
         pl.semaphore_signal(barrier, inc=1, device_id=(other, rep), device_id_type=MESH)
+
+    @pl.when(me > 0)
+    def _():
+        pl.semaphore_signal(barrier, inc=1, device_id=(left, rep), device_id_type=MESH)
+
+    @pl.when(me < leaves - 1)
+    def _():
+        pl.semaphore_signal(barrier, inc=1, device_id=(right, rep), device_id_type=MESH)
+
     for step in range(1, reps):
         other = lax.rem(rep + step, reps)
         pl.semaphore_signal(barrier, inc=1, device_id=(me, other), device_id_type=MESH)
-    for fetch in fetches[:5]:
+    for fetch in fetches[:7]:
         fetch.wait()
 
     tiles_of(bottom, CL_DEV, lines)
@@ -239,6 +247,14 @@
     own_two = packed(lines, 0)
     twos = natural_pair(own_two, own_two, page)[:, :RANK]
 
+    tiles_of(three, chunk, lines_three)
+    place = lax.rem(me // 2, chunk)
+    threes = []
+    for u in range(GROUP // 2):
+        matrix = packed(lines_three, flipped(place, u))
+        threes.append(natural_pair(matrix, matrix, page)[:, :RANK])
+    visits_v[...] = visit_order(admissible, me, padded_in, blocks, fours)
+
     for c in range(CL_DEV):
         half = slice(c % 2 * RANK, c % 2 * RANK + RANK)
         image = exact_dot(leaf_pairs[c // 2][:, half], zero_pairs[c // 2][:, half])
@@ -250,9 +266,10 @@
         transfer = ones[:, i * RANK : (i + 1) * RANK]
         level_two = level_two + exact_gram(transfer, exact_dot(level_one[i], transfer))
     near[1, RANK:, :] = pack(level_two)
-    tops[0] = pack(exact_gram(twos, exact_dot(level_two, twos)))
-
-    pl.semaphore_wait(barrier, GROUP + reps)
+
+    at_edge = (me == 0) | (me == leaves - 1)
+    pl.when(at_edge)(lambda: pl.semaphore_wait(barrier, GROUP + reps - 1))
+    pl.when(jnp.logical_not(at_edge))(lambda: pl.semaphore_wait(barrier, GROUP + reps))
     copies = []
 
     def push(source, target, device):
@@ -261,20 +278,24 @@
             src_ref=source, dst_ref=target, send_sem=send.at[place], recv_sem=receive.at[place],
             device_id=(device, rep), device_id_type=MESH,
         )
-        copy.start()
         copies.append(copy)
-
-    for bits in range(1, GROUP):
-        push(tops.at[0], tops.at[bits], others[bits - 1])
+        return copy
+
     push(near.at[1], near.at[2], left)
     push(near.at[1], near.at[0], right)
+    pl.when(me > 0)(copies[0].start)
+    pl.when(me < leaves - 1)(copies[1].start)
+    tops[0] = pack(exact_gram(twos, exact_dot(level_two, twos)))
+
+    to_scalar = pltpu.make_async_copy(visits_v, order, order_sem)
+    to_scalar.start()
+    for bits in range(1, GROUP):
+        push(tops.at[0], tops.at[bits], others[bits - 1]).start()
     push(factors.at[1], factors.at[2], left)
     push(factors.at[1], factors.at[0], right)
-
-    fetches[6].wait()
-    visits_v[...] = visit_order(admissible, me, padded_in, blocks, pairs)
-    to_scalar = pltpu.make_async_copy(visits_v, order, order_sem)
-    to_scalar.start()
+    pl.when(me > 0)(copies[-2].start)
+    pl.when(me < leaves - 1)(copies[-1].start)
+
     fetches[7].wait()
     own[0] = jnp.zeros((HALF, LANES), BF16)
     turned[0] = jnp.zeros((HALF, LANES), BF16)
@@ -294,14 +315,7 @@
 
     lax.fori_loop(0, blocks // 16, lay, 0, unroll=2)
 
-    fetches[5].wait()
-    tiles_of(three, chunk, lines_three)
-    place = lax.rem(me // 2, chunk)
-    threes = []
-    for u in range(GROUP // 2):
-        matrix = packed(lines_three, flipped(place, u))
-        threes.append(natural_pair(matrix, matrix, page)[:, :RANK])
-    for copy in copies[: GROUP - 1]:
+    for copy in copies[2 : GROUP + 1]:
         copy.wait_recv()
     level_three, lifted = [], []
     for u in range(GROUP // 2):
@@ -309,8 +323,19 @@
         level_three.append(gram)
         lifted.append(exact_gram(threes[u], exact_dot(gram, threes[u])))
     level_four = [lifted[0] + lifted[1], lifted[2] + lifted[3]]
-    for copy in copies[GROUP - 1 :]:
-        copy.wait_recv()
+    pl.when(me < leaves - 1)(copies[0].wait_recv)
+    pl.when(me > 0)(copies[1].wait_recv)
+
+    @pl.when(me == 0)
+    def _():
+        near[0] = near[1]
+        factors[0] = factors[1]
+
+    @pl.when(me == leaves - 1)
+    def _():
+        near[2] = near[1]
+        factors[2] = factors[1]
+
     for side in range(3):
         grams[side * PITCH : side * PITCH + RANK, :] = near[side, :RANK, :]
     side_two = [unpack(near[side, RANK:, :]) for side in range(3)]
@@ -327,6 +352,8 @@
     spread = jnp.where(inner < HALF, 2 * inner, 2 * inner - (RANK - 1)) + (lane - inner)
 
     factorize(grams, upper, 7)
+    pl.when(me < leaves - 1)(copies[-2].wait_recv)
+    pl.when(me > 0)(copies[-1].wait_recv)
 
     def put_column(where, left, right):
         column_left[where] = left.astype(BF16)
@@ -373,58 +400,62 @@
     for k, names in ((1, (4, 5)), (3, (None, 6)), (4, (None, 7)), (5, (None, 8))):
         put_rows(upper[pl.ds(k, HALF, stride=16), :], upper[pl.ds(8 + k, HALF, stride=16), :], names)
 
-    snapshots[pairs] = jnp.zeros((RANK, LANES), F32)
+    snapshots[fours] = jnp.zeros((RANK, LANES), F32)
     to_scalar.wait()
 
-    def visits(step, carry):
-        places = [step * BATCH + k for k in range(BATCH)]
-        halves = []
-        for pair in places:
-            a, b = order[0, 2 * pair], order[0, 2 * pair + 1]
-            both = jnp.concatenate(
+    halves = []
+    for four in range(fours):
+        sides = []
+        for k in range(4 * four, 4 * four + 4, 2):
+            a, b = order[0, k], order[0, k + 1]
+            sides.append(jnp.concatenate(
                 [jnp.where(side, own[a], turned[b]), jnp.where(side, turned[a], own[b])], axis=0
+            ))
+        row = row_table[order[2, 4 * four]][:, :RANK]
+        halves.append(
+            jnp.dot(row, jnp.concatenate(sides, axis=1), preferred_element_type=F32).astype(BF16)
+        )
+    products = []
+    for four, half in enumerate(halves):
+        for k in range(2):
+            at = 4 * four + 2 * k
+            columns = jnp.concatenate(
+                [column_left[order[1, at]], column_right[order[1, at + 1]]], axis=0
             )
-            slot = order[2, 2 * pair]
-            halves.append(
-                jnp.dot(row_table[slot][:, :RANK], both, preferred_element_type=F32).astype(BF16)
-            )
-        products = []
-        for pair, half in zip(places, halves):
-            columns = jnp.concatenate(
-                [column_left[order[1, 2 * pair]], column_right[order[1, 2 * pair + 1]]], axis=0
-            )
-            products.append(jnp.dot(half, columns, preferred_element_type=F32))
-        terms = []
-        for product in products:
-            rounded = product.astype(BF16)
-            terms.append(lax.dot_general(
-                rounded, rounded, (((1,), (1,)), ((), ())), preferred_element_type=F32
-            ))
-        for pair, result in zip(places, products):
-            top, bottom_half = result[:HALF], result[HALF:]
-            results[2 * pair] = jnp.where(side, top, swap(bottom_half))
-            results[2 * pair + 1] = jnp.where(side, swap(top), bottom_half)
-        for pair, term in zip(places, terms):
-            carry = carry * order[3, 2 * pair].astype(F32) + term
-            snapshots[pair, :, :RANK] = carry
-        return carry
-
-    lax.fori_loop(0, pairs // BATCH, visits, jnp.zeros((RANK, RANK), F32))
+            span = slice(k * LANES, (k + 1) * LANES)
+            products.append(jnp.dot(half[:, span], columns, preferred_element_type=F32))
+    terms = []
+    for four in range(fours):
+        rounded = jnp.concatenate(products[2 * four : 2 * four + 2], axis=1).astype(BF16)
+        terms.append(lax.dot_general(
+            rounded, rounded, (((1,), (1,)), ((), ())), preferred_element_type=F32
+        ))
+    for pair, result in enumerate(products):
+        top, bottom_half = result[:HALF], result[HALF:]
+        results[2 * pair] = jnp.where(side, top, swap(bottom_half))
+        results[2 * pair + 1] = jnp.where(side, swap(top), bottom_half)
+    running = jnp.zeros((RANK, RANK), F32)
+    for four, term in enumerate(terms):
+        running = running * order[3, 4 * four].astype(F32) + term
+        snapshots[four, :, :RANK] = running
 
     gather = jnp.where(inner % 2 == 0, inner // 2, HALF + inner // 2)
     for s in range(SLOTS):
         x = picked(snapshots[order[4, s]], gather)
         part = jnp.where(side, x[:HALF], x[HALF:]) * (1.0 / RANK)
-        parts[rep, s * HALF : (s + 1) * HALF, :] = part.astype(BF16)
+        share[s * HALF : (s + 1) * HALF, :] = part.astype(BF16)
     shares = []
     for step in range(1, reps):
         copy = pltpu.make_async_remote_copy(
-            src_ref=parts.at[rep], dst_ref=parts.at[rep],
+            src_ref=share, dst_ref=parts_to.at[rep],
             send_sem=share_send.at[step - 1], recv_sem=share_receive.at[step - 1],
             device_id=(me, lax.rem(rep + step, reps)), device_id_type=MESH,
         )
         copy.start()
         shares.append(copy)
+
+    own_share = pltpu.make_async_copy(share, parts_to.at[rep], stored.at[blocks // 16])
+    own_share.start()
 
     def store_of(group):
         span = pl.ds(pl.multiple_of(group * 16, 16), 16)
@@ -450,45 +481,32 @@
     lax.fori_loop(0, groups, write, 0)
     for copy in shares:
         copy.wait_recv()
-    added_up = parts[0].astype(F32)
-    for k in range(1, reps):
-        added_up = added_up + parts[k].astype(F32)
-    for s in range(SLOTS):
-        total[s * APART : s * APART + HALF, :] = added_up[s * HALF : (s + 1) * HALF]
-    for tile in range(HALF):
-        span = slice(tile * LANES, (tile + 1) * LANES)
-        zero_v[:, span] = total[pl.ds(tile, CL_DEV, stride=APART), :]
-        one_v[:, span] = total[pl.ds(tile + CL_DEV * APART, CL_DEV // 2, stride=APART), :]
-        at = tile + (SLOTS - 1) * APART
-        two_v[:, span] = total[at : at + 1, :]
-    stores = [
-        pltpu.make_async_copy(source, target, stored.at[groups + k])
-        for k, (source, target) in enumerate(
-            ((zero_v, weights_zero), (one_v, weights_one), (two_v, weights_two))
-        )
-    ]
-    for store in stores:
-        store.start()
-    for copy in copies + shares:
+    for copy in copies[2 : GROUP + 1] + shares:
         copy.wait_send()
-    for store in stores + [store_of(group) for group in range(groups)]:
-        store.wait()
+    pl.when(me > 0)(copies[0].wait_send)
+    pl.when(me < leaves - 1)(copies[1].wait_send)
+    pl.when(me > 0)(copies[-2].wait_send)
+    pl.when(me < leaves - 1)(copies[-1].wait_send)
+    own_share.wait()
+    for group in range(groups):
+        store_of(group).wait()
 
 
 def main_call(leaves, reps, order, bottom, zero, one, two, three, admissible, coupling):
     chunk = min(8, three.shape[0])
     blocks = coupling.shape[0]
-    pairs = (blocks + ROW_SLOTS) // 2
-    pairs = -(-pairs // BATCH) * BATCH
+    fours = (blocks + 3 * ROW_SLOTS) // 4
     hbm = pl.BlockSpec(memory_space=pltpu.HBM)
-    small = [jax.ShapeDtypeStruct((count, FLAT), F32) for count in (CL_DEV, CL_DEV // 2, 1)]
     count = GROUP + 3
     whole = [bottom, zero, one, two]
     return pl.pallas_call(
-        functools.partial(main_kernel, leaves, reps, blocks, chunk, pairs),
-        out_shape=[jax.ShapeDtypeStruct((blocks, FLAT), BF16)] + small,
+        functools.partial(main_kernel, leaves, reps, blocks, chunk, fours),
+        out_shape=[
+            jax.ShapeDtypeStruct((blocks, FLAT), BF16),
+            jax.ShapeDtypeStruct((reps, SLOTS * HALF, LANES), BF16),
+        ],
         in_specs=[hbm] * 8,
-        out_specs=[hbm] * 4,
+        out_specs=[hbm] * 2,
         scratch_shapes=[
             pltpu.SMEM(order.shape, jnp.int32),
             *[pltpu.VMEM(x.shape, x.dtype) for x in whole],
@@ -496,7 +514,6 @@
             pltpu.VMEM(admissible.shape, jnp.int32),
             pltpu.VMEM(coupling.shape, BF16),
             pltpu.VMEM(coupling.shape, BF16),
-            *[pltpu.VMEM(x.shape, F32) for x in small],
             pltpu.VMEM((640, LANES), F32),
             pltpu.VMEM((HALF * 8, LANES), F32),
             pltpu.VMEM((RANK, LANES), F32),
@@ -514,12 +531,11 @@
             pltpu.VMEM((COLUMNS, RANK, LANES), BF16),
             pltpu.VMEM((blocks + 1, HALF, LANES), BF16),
             pltpu.VMEM((blocks + 1, HALF, LANES), BF16),
-            pltpu.VMEM((2 * pairs, HALF, LANES), F32),
-            pltpu.VMEM((pairs + 1, RANK, LANES), F32),
-            pltpu.VMEM((reps, SLOTS * HALF, LANES), BF16),
-            pltpu.VMEM((SLOTS * APART, LANES), F32),
+            pltpu.VMEM((4 * fours, HALF, LANES), F32),
+            pltpu.VMEM((fours + 1, RANK, LANES), F32),
+            pltpu.VMEM((SLOTS * HALF, LANES), BF16),
             pltpu.SemaphoreType.DMA((8,)),
-            pltpu.SemaphoreType.DMA((blocks // 16 + 3,)),
+            pltpu.SemaphoreType.DMA((blocks // 16 + 1,)),
             pltpu.SemaphoreType.DMA,
             pltpu.SemaphoreType.DMA((count,)),
             pltpu.SemaphoreType.DMA((count,)),
@@ -533,44 +549,66 @@
     )(order, bottom, zero, one, two, three, admissible, coupling)
 
 
-def deliver_kernel(parts, *refs):
-    count = len(refs) // 3
-    sources, targets, held = refs[:count], refs[count : 2 * count], refs[2 * count : 3 * count]
-    came, went = refs[3 * count :]
-    rows = sources[0].shape[0] // parts
-    spans = [(0, pl.ds(k * rows, rows)) for k in range(parts)]
-    spans += [(k, pl.ds(0, sources[k].shape[0])) for k in range(1, count)]
+def deliver_kernel(
+    parts, projected_in, shares_in, projected_to, zero_to, one_to, two_to,
+    projected, shares, total, zero, one, two, came, went,
+):
+    rows = projected.shape[0] // parts
+    spans = [pl.ds(k * rows, rows) for k in range(parts)]
     reads = [
-        pltpu.make_async_copy(sources[k].at[span], held[k].at[span], came.at[n])
-        for n, (k, span) in enumerate(spans)
+        pltpu.make_async_copy(projected_in.at[span], projected.at[span], came.at[k])
+        for k, span in enumerate(spans)
     ]
     writes = [
-        pltpu.make_async_copy(held[k].at[span], targets[k].at[span], went.at[n])
-        for n, (k, span) in enumerate(spans)
+        pltpu.make_async_copy(projected.at[span], projected_to.at[span], went.at[k])
+        for k, span in enumerate(spans)
     ]
-    for read in reads:
+    fetch = pltpu.make_async_copy(shares_in, shares, came.at[parts])
+    for read in reads[:1] + [fetch] + reads[1:]:
         read.start()
     for read, write in zip(reads, writes):
         read.wait()
         write.start()
+    fetch.wait()
+    summed = shares[0].astype(F32)
+    for k in range(1, shares.shape[0]):
+        summed = summed + shares[k].astype(F32)
+    for s in range(SLOTS):
+        total[s * APART : s * APART + HALF, :] = summed[s * HALF : (s + 1) * HALF]
+    for tile in range(HALF):
+        span = slice(tile * LANES, (tile + 1) * LANES)
+        zero[:, span] = total[pl.ds(tile, CL_DEV, stride=APART), :]
+        one[:, span] = total[pl.ds(tile + CL_DEV * APART, CL_DEV // 2, stride=APART), :]
+        at = tile + (SLOTS - 1) * APART
+        two[:, span] = total[at : at + 1, :]
+    for k, (source, target) in enumerate(((zero, zero_to), (one, one_to), (two, two_to))):
+        writes.append(pltpu.make_async_copy(source, target, went.at[parts + k]))
+        writes[-1].start()
     for write in writes:
         write.wait()
 
 
-def deliver_call(*arrays):
+def deliver_call(projected, shares):
     hbm = pl.BlockSpec(memory_space=pltpu.HBM)
     parts = 4
-    moves = len(arrays) - 1 + parts
+    small = [(count, FLAT) for count in (CL_DEV, CL_DEV // 2, 1)]
     return pl.pallas_call(
         functools.partial(deliver_kernel, parts),
-        out_shape=[jax.ShapeDtypeStruct(x.shape, x.dtype) for x in arrays],
-        in_specs=[hbm] * len(arrays),
-        out_specs=[hbm] * len(arrays),
-        scratch_shapes=[pltpu.VMEM(x.shape, x.dtype) for x in arrays]
-        + [pltpu.SemaphoreType.DMA((moves,))] * 2,
+        out_shape=[jax.ShapeDtypeStruct(projected.shape, BF16)]
+        + [jax.ShapeDtypeStruct(shape, F32) for shape in small],
+        in_specs=[hbm] * 2,
+        out_specs=[hbm] * 4,
+        scratch_shapes=[
+            pltpu.VMEM(projected.shape, BF16),
+            pltpu.VMEM(shares.shape, BF16),
+            pltpu.VMEM((SLOTS * APART, LANES), F32),
+            *[pltpu.VMEM(shape, F32) for shape in small],
+            pltpu.SemaphoreType.DMA((parts + 1,)),
+            pltpu.SemaphoreType.DMA((parts + 3,)),
+        ],
         compiler_params=pltpu.CompilerParams(vmem_limit_bytes=60 * MIB),
         name="deliver",
-    )(*arrays)
+    )(projected, shares)
 
 
 def local(leaves, reps, bottom, zero, one, two, three, order, coupling, admissible):

time: 31.6 us -> 30.5 us (0.965)
  the two profiles are of different devices: /device:TPU:2 before, /device:TPU:8 now
where the time goes in v5:
time: 30.5 us; the launch traced here: 30.3 us
  Pallas kernels  29.7 us (97%)
  between operations  0.64 us (2%)
    pallas_call x1, Pallas kernels, main_call(): pl.pallas_call(functools.partial(main_kernel, leaves, reps, blocks, chunk...  27.3 us
    pallas_call x1, Pallas kernels, deliver_call(): pl.pallas_call(functools.partial(deliver_kernel, parts), out_shape=[jax.S...  2.35 us

profile of v5, /device:TPU:8, one launch (start us, length us, event | category | flops | bytes accessed | tf_op | source)
XLA Modules:
  0.0 30.3 jit_solution(10991821940792851510)
XLA Ops:
  0.6 27.3 %upsweep_and_blocks.1 = (bf16[192,4096]{1,0:T(8,128)(2,1)}, bf16[4,224,128]{2,1,0:T(8,128)(2,1)}) custom-call(s32[1,4]{1,0:T(1,128)} %order_in.1, f32[4,4096]{1,0:T(4,128)} %bottom_in.1, f32[4,4096]{1,0:T(4,128)} %zero_in.1, f32[2,4096]{1,0:T(2,128)} %one_in.1, f32[1,4096]{1,0:T(1,128)} %two_in.1, f32[64,4096]{1,0:T(8,128)} %three_in.1, ...), custom_call_target="tpu_custom_call" | custom-call | tf_op jit(solution)/shard_map/upsweep_and_blocks/pallas_call | solution.py:502
  27.9 2.4 %deliver.1 = (bf16[192,4096]{1,0:T(8,128)(2,1)}, f32[4,4096]{1,0:T(4,128)}, f32[2,4096]{1,0:T(2,128)}, f32[1,4096]{1,0:T(1,128)}) custom-call(bf16[192,4096]{1,0:T(8,128)(2,1)} %get-tuple-element.6.projected_in, bf16[4,224,128]{2,1,0:T(8,128)(2,1)} %get-tuple-element.7.shares_in), custom_call_target="tpu_custom_call" | custom-call | tf_op jit(solution)/shard_map/deliver/pallas_call | solution.py:595
